TPU v7x, 256 devices: a whole 4x4x8 slice. The times are simulated.
256 devices in a mesh: dp: 4 (over x), ctx: 32 (over y, z_lo, core), chan: 2 (over z_hi).
Axes of the slice: x: 4, y: 4, z: 8 (z_hi: 2, z_lo: 4; z = z_hi * 4 + z_lo), core: 2. Of those that a mesh axis runs over, the one named last changes fastest.
Arguments:
- queries: bfloat16 [4, 4096, 2048], P('dp', 'ctx', 'chan'), may hold values from -6 to 6
- keys_raw: bfloat16 [4, 4096, 2048], P('dp', 'ctx', 'chan'), may hold values from -6 to 6
- values: bfloat16 [4, 4096, 2048], P('dp', 'ctx', 'chan'), may hold values from -6 to 6
- grad_out: bfloat16 [4, 4096, 2048], P('dp', 'ctx', 'chan'), may hold values from -6 to 6
- short_filter: float32 [3, 2048], P(None, 'chan'), may hold values from -3 to 3
- long_filter: float32 [4096, 2048], P('ctx', 'chan'), may hold values from -6 to 6
- skip_gain: float32 [2048], P('chan'), may hold values from -4 to 4
Outputs:
- grad_queries: bfloat16 [4, 4096, 2048], P('dp', 'ctx', 'chan')
- grad_keys_raw: bfloat16 [4, 4096, 2048], P('dp', 'ctx', 'chan')
- grad_values: bfloat16 [4, 4096, 2048], P('dp', 'ctx', 'chan')
- grad_long: float32 [4096, 2048], P('ctx', 'chan')
- grad_short: float32 [3, 2048], P(None, 'chan')
- grad_skip: float32 [2048], P('chan')
All inputs are finite; a program needn't handle non-finite values.
Results may differ from a plain program's by a relative error of at most 0.001.
Values may be sent and summed in bfloat16 or wider, within the bound.
A program may use at most 64 MiB of HBM per device.

v0:
```python
import math

import jax
import jax.numpy as jnp
from jax import lax
from jax.sharding import PartitionSpec as P


def passed_along(value, axis, steps):
    count = lax.axis_size(axis)
    first, last = (max(0, -steps), min(count, count - steps))
    return lax.ppermute(value, axis, [(source, source + steps) for source in range(first, last)])


def first_factor(length):
    for factor in range(min(length, 128), 1, -1):
        if length % factor == 0:
            return factor
    return length


def angle_pair(left_count, right_count, length, sign):
    left_side = jnp.arange(left_count, dtype=jnp.int32)
    right_side = jnp.arange(right_count, dtype=jnp.int32)
    phases = left_side[:, None] * right_side[None, :] % length
    angles = phases.astype(jnp.float32) * (2.0 * math.pi / length)
    return (jnp.cos(angles), sign * jnp.sin(angles))


def block_table(left_count, right_count, length, sign):
    cosine, sine = angle_pair(left_count, right_count, length, sign)
    from_real = jnp.stack([cosine, sine], axis=1)
    from_imag = jnp.stack([-sine, cosine], axis=1)
    return jnp.stack([from_real, from_imag], axis=0)


def transform(parts, length, sign):
    have = parts.shape[-1]
    leading = parts.shape[1:-1]
    factor = first_factor(length)
    if factor == length:
        table = block_table(have, length, length, sign)
        return jnp.einsum("c...a,cadk->d...k", parts, table, precision=lax.Precision.HIGHEST)
    remain = length // factor
    rows = have // remain
    split = parts.reshape((2,) + leading + (rows, remain))
    table = block_table(rows, factor, factor, sign)
    section = jnp.einsum("c...ab,cadk->d...kb", split, table, precision=lax.Precision.HIGHEST)
    twist_cos, twist_sin = angle_pair(factor, remain, length, sign)
    turned = jnp.stack(
        [
            section[0] * twist_cos - section[1] * twist_sin,
            section[0] * twist_sin + section[1] * twist_cos,
        ]
    )
    inner = transform(turned, remain, sign)
    return jnp.swapaxes(inner, -1, -2).reshape((2,) + leading + (length,))


def spectral(gated_seq, upstream_seq, filter_seq):
    full_tokens = gated_seq.shape[-1]
    full_length = 2 * full_tokens
    mixed = transform(jnp.stack([gated_seq, upstream_seq]), full_length, -1.0)
    mixed_real, mixed_imag = (mixed[0], mixed[1])
    flipped_real = jnp.roll(jnp.flip(mixed_real, -1), 1, -1)
    flipped_imag = jnp.roll(jnp.flip(mixed_imag, -1), 1, -1)
    gate_real = 0.5 * (mixed_real + flipped_real)
    gate_imag = 0.5 * (mixed_imag - flipped_imag)
    grad_real = 0.5 * (mixed_imag + flipped_imag)
    grad_imag = 0.5 * (flipped_real - mixed_real)
    filt = transform(jnp.stack([filter_seq, jnp.zeros_like(filter_seq)]), full_length, -1.0)
    filt_real, filt_imag = (filt[0], filt[1])
    ahead_real = gate_real * filt_real - gate_imag * filt_imag
    ahead_imag = gate_real * filt_imag + gate_imag * filt_real
    behind_real = filt_real * grad_real + filt_imag * grad_imag
    behind_imag = filt_real * grad_imag - filt_imag * grad_real
    cross_real = gate_real * grad_real + gate_imag * grad_imag
    cross_imag = gate_real * grad_imag - gate_imag * grad_real
    stacked = jnp.stack(
        [
            jnp.stack([ahead_real - behind_imag, cross_real]),
            jnp.stack([ahead_imag + behind_real, cross_imag]),
        ]
    )
    results = transform(stacked, full_length, 1.0)
    conv_rows = results[0, 0, :, :full_tokens] / full_length
    back_seq = results[1, 0, :, :full_tokens] / full_length
    lag_seq = results[0, 1, :, :full_tokens] / full_length
    return (conv_rows, back_seq, lag_seq)


def to_groups(token_rows, context):
    tokens_here, width = token_rows.shape
    return token_rows.T.reshape(context, width // context, tokens_here)


def from_groups(blocks):
    context, group_width, tokens_here = blocks.shape
    return blocks.reshape(context * group_width, tokens_here).T


def per_device(queries, keys_raw, values, grad_out, short_filter, long_filter, skip_gain):
    context = lax.axis_size("ctx")
    replicas = lax.axis_size("dp")
    tokens_here = queries.shape[1]
    full_tokens = tokens_here * context
    grad_scale = 1.0 / math.sqrt(replicas * full_tokens)
    raw_rows = keys_raw[0].astype(jnp.float32)
    earlier = passed_along(keys_raw[:, tokens_here - 2 :, :], "ctx", 1)
    extended = jnp.concatenate([earlier[0].astype(jnp.float32), raw_rows], axis=0)
    tap_zero = short_filter[0]
    tap_one = short_filter[1]
    tap_two = short_filter[2]
    key_rows = tap_zero * extended[2:] + tap_one * extended[1:-1] + tap_two * extended[:-2]
    value_rows = values[0].astype(jnp.float32)
    gated_rows = key_rows * value_rows
    grad_rows = grad_out[0].astype(jnp.float32)
    upstream = grad_rows * queries[0].astype(jnp.float32)
    gated_blocks = to_groups(gated_rows, context)
    upstream_blocks = to_groups(upstream, context)
    filter_blocks = to_groups(long_filter, context)
    gated_chan, upstream_chan, filter_chan = (
        lax.all_to_all(gated_blocks, "ctx", split_axis=0, concat_axis=2, tiled=True),
        lax.all_to_all(upstream_blocks, "ctx", split_axis=0, concat_axis=2, tiled=True),
        lax.all_to_all(filter_blocks, "ctx", split_axis=0, concat_axis=2, tiled=True),
    )
    conv_chan, back_chan, lag_chan = spectral(gated_chan[0], upstream_chan[0], filter_chan[0])
    conv_home, back_home, lag_home = (
        lax.all_to_all(conv_chan[None], "ctx", split_axis=2, concat_axis=0, tiled=True),
        lax.all_to_all(back_chan[None], "ctx", split_axis=2, concat_axis=0, tiled=True),
        lax.all_to_all(lag_chan[None], "ctx", split_axis=2, concat_axis=0, tiled=True),
    )
    lag_total = lax.psum(lag_home, "dp")
    grad_long = from_groups(lag_total) * grad_scale
    conv_rows = from_groups(conv_home)
    back_rows = from_groups(back_home)
    grad_queries = (grad_rows * (conv_rows + skip_gain * gated_rows)).astype(jnp.bfloat16)
    grad_gated = back_rows + skip_gain * upstream
    grad_values = (grad_gated * key_rows).astype(jnp.bfloat16)
    grad_key_rows = grad_gated * value_rows
    later_rows = passed_along(grad_key_rows[:2][None], "ctx", -1)
    after = jnp.concatenate([grad_key_rows, later_rows[0]], axis=0)
    grad_keys_raw = (tap_zero * grad_key_rows + tap_one * after[1:-1] + tap_two * after[2:]).astype(
        jnp.bfloat16
    )
    short_terms = jnp.stack(
        [
            jnp.sum(grad_key_rows * extended[2:], axis=0),
            jnp.sum(grad_key_rows * extended[1:-1], axis=0),
            jnp.sum(grad_key_rows * extended[:-2], axis=0),
        ]
    )
    skip_terms = jnp.sum(upstream * gated_rows, axis=0)
    short_total, skip_total = lax.psum((short_terms, skip_terms), ("dp", "ctx"))
    return (
        grad_queries[None],
        grad_keys_raw[None],
        grad_values[None],
        grad_long,
        short_total * grad_scale,
        skip_total * grad_scale,
    )


def solution(mesh):
    return jax.shard_map(
        per_device,
        mesh=mesh,
        in_specs=(
            P("dp", "ctx", "chan"),
            P("dp", "ctx", "chan"),
            P("dp", "ctx", "chan"),
            P("dp", "ctx", "chan"),
            P(None, "chan"),
            P("ctx", "chan"),
            P("chan"),
        ),
        out_specs=(
            P("dp", "ctx", "chan"),
            P("dp", "ctx", "chan"),
            P("dp", "ctx", "chan"),
            P("ctx", "chan"),
            P(None, "chan"),
            P("chan"),
        ),
        check_vma=False,
    )
```

profile of v0, /device:TPU:1, one launch (start us, length us, event | category | flops | bytes accessed | tf_op | source)
XLA Modules:
  0.0 972.3 jit_solution(13893810224442208397)
XLA Ops:
  7.2 2.1 copy.249
  9.3 10.3 %all-to-all-start.2 = ((f32[32,32,128]{2,1,0:T(8,128)}), f32[32,32,128]{2,1,0:T(8,128)S(1)}, u32[]{:S(2)}, u32[]{:S(2)}) async-start(f32[32,32,128]{2,1,0:T(8,128)} %bitcast.50), calls=%async_computation.2 | async-start | bytes 1048576 | tf_op jit(solution)/shard_map/all_to_all | solution.py:125
  19.9 3.5 collective-permute-start
  24.3 7.2 collective-permute-done
  32.3 2.6 multiply_reduce_fusion
  34.9 4.3 all-to-all-done.2
  39.2 6.3 all-to-all-start
  46.8 15.6 %all-to-all-done = f32[32,32,128]{2,1,0:T(8,128)S(1)} async-done(((f32[32,32,128]{2,1,0:T(8,128)}), f32[32,32,128]{2,1,0:T(8,128)S(1)}, u32[]{:S(2)}, u32[]{:S(2)}) %all-to-all-start) | async-done | bytes 524320 | tf_op jit(solution)/shard_map/all_to_all | solution.py:123
  62.4 4.6 all-to-all-start.1
  72.0 4.9 fusion.28
  77.7 6.0 all-to-all-done.1
  87.5 2.2 multiply_subtract_fusion.3
  89.7 2.2 fusion.25
  99.1 4.6 reverse.4
  106.9 4.6 reverse.5
  112.3 2.2 concatenate.61
  114.5 3.3 copy.248
  119.4 3.3 copy.256
  122.8 2.0 fusion.31
  126.9 3.2 squeeze.19
  130.0 2.3 copy.258
  132.3 2.7 subtract_subtract_fusion
  136.0 3.4 fusion.13
  140.4 5.5 fusion.10
  146.0 4.9 reshape.788
  150.9 2.3 fusion.42
  153.2 2.4 copy.271
  156.2 19.6 %reduce.2 = f32[4096,32]{1,0:T(8,128)} reduce(f32[4096,1,32]{2,1,0:T(1,128)S(1)} %bitcast.254, f32[]{:T(128)} %broadcast.758), dimensions={1}, to_apply=%bitcast.231.reduce_sub_computation | reduce | bytes 1048580
  175.7 3.1 reshape.813
  178.8 3.7 all-to-all-start.3
  182.6 4.7 copy.274
  187.2 19.4 %reduce = f32[4096,32]{1,0:T(8,128)} reduce(f32[4096,1,32]{2,1,0:T(1,128)S(1)} %bitcast.255, f32[]{:T(128)} %broadcast.758), dimensions={1}, to_apply=%bitcast.233.reduce_sub_computation | reduce | bytes 1048580
  206.6 3.1 reshape.815
  209.7 8.3 all-to-all-start.4
  218.0 2.5 copy.277
  220.5 19.4 %reduce.4 = f32[4096,32]{1,0:T(8,128)} reduce(f32[4096,1,32]{2,1,0:T(1,128)S(1)} %bitcast.256, f32[]{:T(128)} %broadcast.758), dimensions={1}, to_apply=%bitcast.235.reduce_sub_computation | reduce | bytes 1048580
  239.9 3.1 reshape.817
  243.0 7.7 all-to-all-start.5
  252.7 3.5 reshape.814
  258.8 2.9 reduce.1
  261.7 3.5 reshape.816
  265.3 3.2 copy.275
  269.9 3.0 multiply_reduce_fusion.2
  274.5 2.9 reduce.5
  277.5 3.5 reshape.818
  281.0 3.2 copy.278
  284.3 663.3 %all-reduce.1 = (f32[3,1024]{1,0:T(4,128)S(1)}, f32[1024]{0:T(1024)S(1)}) all-reduce(f32[3,1024]{1,0:T(4,128)S(1)} %pad_maximum_fusion.11, f32[1024]{0:T(1024)S(1)} %copy-done.40), channel_id=1, replica_groups=mesh['dp'=4,'ctx'=32,'chan'=2] {'dp','ctx'}, use_global_device_ids=true, to_apply=%region_4.5 | all-reduce | flops 4096 | bytes 32768 | tf_op jit(solution)/shard_map/psum | solution.py:154
  948.2 10.2 %collective-permute-start.1 = (f32[1,2,1024]{1,2,0:T(8,128)}, f32[1,2,1024]{1,2,0:T(8,128)S(1)}, u32[]{:S(2)}, u32[]{:S(2)}) collective-permute-start(f32[1,2,1024]{1,2,0:T(8,128)} %slice_bitcast_fusion), channel_id=1, source_target_pairs={{2,0},{4,2},{6,4},{8,6},{10,8},{12,10},{14,12},{16,14},{18,16},{20... | collective-permute-start | bytes 24584 | tf_op jit(solution)/shard_map/ppermute | solution.py:12
  (161 shorter events, 44.4 us)
Async XLA Ops:
  7.2 12.5 %copy-start.25 = (bf16[1,128,1024]{2,1,0:T(8,128)(2,1)S(1)}, bf16[1,128,1024]{2,1,0:T(8,128)(2,1)}, u32[]{:S(2)}) copy-start(bf16[1,128,1024]{2,1,0:T(8,128)(2,1)} %param.8) | copy-start | bytes 786436
  7.2 16.5 %copy-start.41 = (f32[3,1024]{1,0:T(4,128)S(1)}, f32[3,1024]{1,0:T(4,128)}, u32[]{:S(2)}) copy-start(f32[3,1024]{1,0:T(4,128)} %param.11) | copy-start | bytes 36868
  7.2 16.5 %copy-start.28 = (bf16[1,128,1024]{2,1,0:T(8,128)(2,1)S(1)}, bf16[1,128,1024]{2,1,0:T(8,128)(2,1)}, u32[]{:S(2)}) copy-start(bf16[1,128,1024]{2,1,0:T(8,128)(2,1)} %param.10) | copy-start | bytes 786436
  7.2 16.7 %copy-start.29 = (bf16[1,128,1024]{2,1,0:T(8,128)(2,1)S(1)}, bf16[1,128,1024]{2,1,0:T(8,128)(2,1)}, u32[]{:S(2)}) copy-start(bf16[1,128,1024]{2,1,0:T(8,128)(2,1)} %param.9) | copy-start | bytes 786436
  9.3 14.8 %copy-start.30 = (bf16[1,128,1024]{2,1,0:T(8,128)(2,1)S(1)}, bf16[1,128,1024]{2,1,0:T(8,128)(2,1)}, u32[]{:S(2)}) copy-start(bf16[1,128,1024]{2,1,0:T(8,128)(2,1)} %param.7) | copy-start | bytes 786436
  9.3 29.9 %all-to-all-start.2 = ((f32[32,32,128]{2,1,0:T(8,128)}), f32[32,32,128]{2,1,0:T(8,128)S(1)}, u32[]{:S(2)}, u32[]{:S(2)}) async-start(f32[32,32,128]{2,1,0:T(8,128)} %bitcast.50), calls=%async_computation.2 | async-start | bytes 1048576 | tf_op jit(solution)/shard_map/all_to_all | solution.py:125
  19.9 11.6 %collective-permute-start = (bf16[1,2,1024]{1,2,0:T(8,128)(2,1)S(1)}, bf16[1,2,1024]{1,2,0:T(8,128)(2,1)S(1)}, u32[]{:S(2)}, u32[]{:S(2)}) collective-permute-start(bf16[1,2,1024]{1,2,0:T(8,128)(2,1)S(1)} %copy.238), channel_id=1, source_target_pairs={{0,2},{2,4},{4,6},{6,8},{8,10},{10,12},{12,14},{14,16},{16,18},{18... | collective-permute-start | bytes 12296 | tf_op jit(solution)/shard_map/ppermute | solution.py:12
  23.6 11.2 %copy-start.2 = (f32[128,1024]{0,1:T(8,128)}, f32[128,1024]{0,1:T(8,128)S(1)}, u32[]{:S(2)}) copy-start(f32[128,1024]{0,1:T(8,128)S(1)} %bitcast_convert_fusion.1) | copy-start | bytes 1572868
  23.7 11.2 %copy-start.34 = (f32[1,1024]{1,0:T(1,128)}, f32[1,1024]{1,0:T(1,128)S(1)}, u32[]{:S(2)}) copy-start(f32[1,1024]{1,0:T(1,128)S(1)} %get-tuple-element.79) | copy-start | bytes 12292
  23.7 11.2 %copy-start.36 = (f32[1,1024]{1,0:T(1,128)}, f32[1,1024]{1,0:T(1,128)S(1)}, u32[]{:S(2)}) copy-start(f32[1,1024]{1,0:T(1,128)S(1)} %get-tuple-element.80) | copy-start | bytes 12292
  23.7 11.2 %copy-start.38 = (f32[1,1024]{1,0:T(1,128)}, f32[1,1024]{1,0:T(1,128)S(1)}, u32[]{:S(2)}) copy-start(f32[1,1024]{1,0:T(1,128)S(1)} %get-tuple-element.81) | copy-start | bytes 12292
  23.9 11.0 %copy-start.12 = (bf16[1,128,1024]{1,2,0:T(8,128)(2,1)}, bf16[1,128,1024]{1,2,0:T(8,128)(2,1)S(1)}, u32[]{:S(2)}) copy-start(bf16[1,128,1024]{1,2,0:T(8,128)(2,1)S(1)} %copy.233) | copy-start | bytes 786436
  24.1 10.8 %copy-start.13 = (bf16[1,128,1024]{1,2,0:T(8,128)(2,1)}, bf16[1,128,1024]{1,2,0:T(8,128)(2,1)S(1)}, u32[]{:S(2)}) copy-start(bf16[1,128,1024]{1,2,0:T(8,128)(2,1)S(1)} %copy.239) | copy-start | bytes 786436
  24.3 10.6 %copy-start.14 = (bf16[1,128,1024]{1,2,0:T(8,128)(2,1)}, bf16[1,128,1024]{1,2,0:T(8,128)(2,1)S(1)}, u32[]{:S(2)}) copy-start(bf16[1,128,1024]{1,2,0:T(8,128)(2,1)S(1)} %copy.241) | copy-start | bytes 786436
  39.2 23.1 %all-to-all-start = ((f32[32,32,128]{2,1,0:T(8,128)}), f32[32,32,128]{2,1,0:T(8,128)S(1)}, u32[]{:S(2)}, u32[]{:S(2)}) async-start(f32[32,32,128]{2,1,0:T(8,128)} %bitcast.27), calls=%async_computation | async-start | bytes 1048576 | tf_op jit(solution)/shard_map/all_to_all | solution.py:123
  62.4 8.0 copy-start.15
  62.4 21.3 %all-to-all-start.1 = ((f32[32,32,128]{2,1,0:T(8,128)}), f32[32,32,128]{2,1,0:T(8,128)}, u32[]{:S(2)}, u32[]{:S(2)}) async-start(f32[32,32,128]{2,1,0:T(8,128)} %bitcast.33), calls=%async_computation.1 | async-start | bytes 1048576 | tf_op jit(solution)/shard_map/all_to_all | solution.py:124
  72.0 4.9 copy-start.16
  85.6 1.9 copy-start.1
  85.6 1.9 copy-start.23
  85.6 1.9 copy-start.32
  87.5 2.2 copy-start.19
  87.5 2.2 copy-start.20
  99.1 5.1 copy-start.33
  105.3 1.6 copy-start.8
  114.5 3.3 copy-start
  119.4 3.3 copy-start.10
  119.4 3.3 copy-start.11
  130.0 2.3 copy-start.9
  136.0 3.5 copy-start.24
  136.0 3.5 copy-start.31
  139.4 1.0 copy-start.26
  139.4 1.0 copy-start.27
  178.8 30.9 %all-to-all-start.3 = ((f32[32,1,4096]{2,1,0:T(1,128)}), f32[32,1,4096]{2,1,0:T(1,128)S(1)}, u32[]{:S(2)}, u32[]{:S(2)}) async-start(f32[32,1,4096]{2,1,0:T(1,128)} %reshape.813), calls=%async_computation.3 | async-start | bytes 1048576 | tf_op jit(solution)/shard_map/all_to_all | solution.py:129
  209.7 33.3 %all-to-all-start.4 = ((f32[32,1,4096]{2,1,0:T(1,128)}), f32[32,1,4096]{2,1,0:T(1,128)}, u32[]{:S(2)}, u32[]{:S(2)}) async-start(f32[32,1,4096]{2,1,0:T(1,128)} %reshape.815), calls=%async_computation.4 | async-start | bytes 1048576 | tf_op jit(solution)/shard_map/all_to_all | solution.py:130
  243.0 31.5 %all-to-all-start.5 = ((f32[32,1,4096]{2,1,0:T(1,128)}), f32[32,1,4096]{2,1,0:T(1,128)}, u32[]{:S(2)}, u32[]{:S(2)}) async-start(f32[32,1,4096]{2,1,0:T(1,128)} %reshape.817), calls=%async_computation.5 | async-start | bytes 1048576 | tf_op jit(solution)/shard_map/all_to_all | solution.py:131
  250.8 711.9 %all-reduce.4.cloned.1.call-start = ((), (), s32[]{:S(2)}) async-start(), calls=%async_computation.6 | async-start | bytes 1048576 | tf_op jit(solution)/shard_map/psum | solution.py:133
  265.2 4.6 copy-start.3
  265.2 4.6 copy-start.5
  265.2 4.6 copy-start.42
  281.0 3.3 copy-start.40
  281.0 678.0 %copy-start.18 = (bf16[128,1024]{0,1:T(8,128)(2,1)S(1)}, bf16[128,1024]{0,1:T(8,128)(2,1)}, u32[]{:S(2)}) copy-start(bf16[128,1024]{0,1:T(8,128)(2,1)} %get-tuple-element.68) | copy-start | bytes 786436
  281.0 678.9 %copy-start.17 = (bf16[1,128,1024]{1,2,0:T(8,128)(2,1)S(1)}, bf16[1,128,1024]{1,2,0:T(8,128)(2,1)}, u32[]{:S(2)}) copy-start(bf16[1,128,1024]{1,2,0:T(8,128)(2,1)} %get-tuple-element.66) | copy-start | bytes 786436
  281.0 679.7 %copy-start.7 = (f32[128,1024]{0,1:T(8,128)S(1)}, f32[128,1024]{0,1:T(8,128)}, u32[]{:S(2)}) copy-start(f32[128,1024]{0,1:T(8,128)} %copy-done.6) | copy-start | bytes 1572868
  281.0 679.7 %copy-start.35 = (f32[1,1024]{1,0:T(1,128)S(1)}, f32[1,1024]{1,0:T(1,128)}, u32[]{:S(2)}) copy-start(f32[1,1024]{1,0:T(1,128)} %copy-done.34) | copy-start | bytes 12292
  281.0 679.7 %copy-start.37 = (f32[1,1024]{1,0:T(1,128)S(1)}, f32[1,1024]{1,0:T(1,128)}, u32[]{:S(2)}) copy-start(f32[1,1024]{1,0:T(1,128)} %copy-done.36) | copy-start | bytes 12292
  281.0 679.7 %copy-start.39 = (f32[1,1024]{1,0:T(1,128)S(1)}, f32[1,1024]{1,0:T(1,128)}, u32[]{:S(2)}) copy-start(f32[1,1024]{1,0:T(1,128)} %copy-done.38) | copy-start | bytes 12292
  948.2 12.5 %collective-permute-start.1 = (f32[1,2,1024]{1,2,0:T(8,128)}, f32[1,2,1024]{1,2,0:T(8,128)S(1)}, u32[]{:S(2)}, u32[]{:S(2)}) collective-permute-start(f32[1,2,1024]{1,2,0:T(8,128)} %slice_bitcast_fusion), channel_id=1, source_target_pairs={{2,0},{4,2},{6,4},{8,6},{10,8},{12,10},{14,12},{16,14},{18,16},{20... | collective-permute-start | bytes 24584 | tf_op jit(solution)/shard_map/ppermute | solution.py:12
  (4 other events, 3.4 us)
Sparse Core Ops, SparseCore 0:
  284.4 46.7 all-reduce.3
where the time goes:
time: 977 us; the launch traced here: 972 us
  blocking collectives  663 us (68%)
  local copies, waits for them, and re-layouts  97 us (10%)
  other arithmetic  88.9 us (9%)
  starting transfers between devices  54.7 us (6%)
  waiting for transfers between devices  33.1 us (3%)
  matrix products  19.9 us (2%)
  between operations  15.4 us (2%)
    psum x1, blocking collectives, per_device(): short_total, skip_total = lax.psum((short_terms, skip_terms), ('dp', 'ctx'))  663 us
    unnamed x3, other arithmetic  58.3 us
    unnamed x106, local copies, waits for them, and re-layouts  39.1 us
  transfers between devices with their start and end apart: 9, of which 4 were waited for; matrix products, arithmetic and copies ran while one was open for 10% of the time, Pallas kernels for 0%

commit v1 on v0

v1 whole, which is shorter than its diff:
```python
import functools
import math

import jax
import jax.numpy as jnp
import ml_dtypes
import numpy as np
from jax import lax
from jax.experimental import pallas as pl
from jax.experimental.pallas import tpu as pltpu
from jax.sharding import PartitionSpec as P

MESH = pl.DeviceIdType.MESH
LANES = 128
PACK = 8


def two_parts(table):
    high = table.astype(ml_dtypes.bfloat16)
    low = (table - high.astype(np.float64)).astype(ml_dtypes.bfloat16)
    return high, low


def tables(blocks, tokens):
    full = blocks * tokens
    shifted = np.arange(blocks) + 0.25
    outer = 2.0 * np.pi * np.outer(shifted, np.arange(blocks)) / blocks
    first = np.concatenate([np.cos(outer), -np.sin(outer)], axis=0)
    last = np.concatenate([np.cos(outer).T, -np.sin(outer).T], axis=1) / full
    twist = 2.0 * np.pi * np.outer(shifted, np.arange(tokens)) / full
    inner = 2.0 * np.pi * np.outer(np.arange(tokens), np.arange(tokens)) / tokens
    cosine, sine = np.cos(inner), np.sin(inner)
    ahead = np.block([[cosine, -sine], [sine, cosine]])
    back = np.block([[cosine, sine], [-sine, cosine]])
    first_high, first_low = two_parts(first)
    last_high, last_low = two_parts(last)
    ahead_high, ahead_low = two_parts(ahead)
    back_high, back_low = two_parts(back)
    return (
        np.concatenate([first_high, first_high, first_low], axis=1),
        np.concatenate([last_high, last_high, last_low], axis=1),
        np.concatenate([ahead_high, ahead_high, ahead_low], axis=0),
        np.concatenate([back_high, back_high, back_low], axis=0),
        np.cos(twist).astype(np.float32),
        np.sin(twist).astype(np.float32),
    )


def split_stack(value, axis):
    high = value.astype(jnp.bfloat16)
    low = (value - high.astype(jnp.float32)).astype(jnp.bfloat16)
    return jnp.concatenate([high, low, high], axis=axis)


def forward(source, target, first, ahead, twist_cos, twist_sin):
    channels, blocks, _ = source.shape

    @pl.loop(0, channels // PACK)
    def _(group):
        base = group * PACK
        rows = jnp.concatenate([source[base + j] for j in range(PACK)], axis=1)
        section = jnp.dot(first[...], split_stack(rows, 0), preferred_element_type=jnp.float32)
        cosine, sine = twist_cos[...], twist_sin[...]
        turned = []
        for j in range(PACK):
            real = section[:blocks, j * LANES : (j + 1) * LANES]
            imag = section[blocks:, j * LANES : (j + 1) * LANES]
            turned.append(jnp.concatenate([real * cosine + imag * sine, imag * cosine - real * sine], axis=1))
        turned = jnp.concatenate(turned, axis=0)
        size = PACK * blocks
        target[pl.ds(pl.multiple_of(group * size, size), size), :] = jnp.dot(
            split_stack(turned, 1), ahead[...], preferred_element_type=jnp.float32
        )


def inverse(left, right, conjugate, target, last, back, twist_cos, twist_sin):
    channels, blocks, _ = target.shape

    @pl.loop(0, channels // PACK)
    def _(group):
        size = PACK * blocks
        rows = pl.ds(pl.multiple_of(group * size, size), size)
        a_real, a_imag = left[rows, :LANES], left[rows, LANES:]
        b_real, b_imag = right[rows, :LANES], right[rows, LANES:]
        if conjugate:
            real, imag = a_real * b_real + a_imag * b_imag, a_real * b_imag - a_imag * b_real
        else:
            real, imag = a_real * b_real - a_imag * b_imag, a_real * b_imag + a_imag * b_real
        product = jnp.concatenate([real, imag], axis=1)
        section = jnp.dot(split_stack(product, 1), back[...], preferred_element_type=jnp.float32)
        cosine, sine = twist_cos[...], twist_sin[...]
        turned = []
        for j in range(PACK):
            real = section[j * blocks : (j + 1) * blocks, :LANES]
            imag = section[j * blocks : (j + 1) * blocks, LANES:]
            turned.append(jnp.concatenate([real * cosine - imag * sine, real * sine + imag * cosine], axis=0))
        turned = jnp.concatenate(turned, axis=1)
        result = jnp.dot(last[...], split_stack(turned, 0), preferred_element_type=jnp.float32)
        for j in range(PACK):
            target[group * PACK + j] = result[:, j * LANES : (j + 1) * LANES]


def kernel(
    context,
    replicas,
    grad_scale,
    queries,
    keys_raw,
    values,
    grad_out,
    short_filter,
    long_filter,
    skip_gain,
    first,
    last,
    ahead,
    back,
    twist_cos,
    twist_sin,
    grad_queries,
    grad_keys_raw,
    grad_values,
    grad_long,
    grad_short,
    grad_skip,
    filter_send,
    upstream_send,
    gated_send,
    filter_seq,
    upstream_seq,
    gated_seq,
    filter_freq,
    upstream_freq,
    gated_freq,
    back_seq,
    conv_seq,
    lag_seq,
    back_home,
    conv_home,
    lag_parts,
    lag_sum,
    lag_home,
    key_edge,
    key_ext,
    key_rows,
    grad_key_ext,
    terms,
    terms_in,
    terms_dp,
    terms_all,
    send_sem,
    recv_sem,
):
    tokens, width = key_rows.shape
    me = lax.axis_index("ctx")
    row = lax.axis_index("dp")
    tiles = width // LANES
    per_tile = LANES // filter_send.shape[2] // filter_send.shape[1]
    following = lax.rem(me + 1, context)
    preceding = lax.rem(me + context - 1, context)

    def over_context(step):
        @pl.loop(1, context)
        def _(i):
            step(lax.rem(me + i, context))

    def over_replicas(step):
        @pl.loop(1, replicas)
        def _(i):
            step(lax.rem(row + i, replicas))

    def push(source, target, number, **peer):
        pltpu.make_async_remote_copy(
            src_ref=source,
            dst_ref=target,
            send_sem=send_sem.at[number],
            recv_sem=recv_sem.at[number],
            device_id=peer,
            device_id_type=MESH,
        ).start()

    def keep(source, target, number):
        pltpu.make_async_copy(source, target, recv_sem.at[number]).start()

    def arrived(extent, number):
        pltpu.make_async_copy(extent, extent, recv_sem.at[number]).wait()

    def sent(extent, number):
        pltpu.make_async_copy(extent, extent, send_sem.at[number]).wait()

    def lane_tiles(step):
        @pl.loop(0, tiles)
        def _(t):
            step(t, pl.ds(pl.multiple_of(t * LANES, LANES), LANES))

    def upstream_of(lanes):
        return grad_out[0, :, lanes].astype(jnp.float32) * queries[0, :, lanes].astype(jnp.float32)

    barrier = pltpu.get_barrier_semaphore()
    over_context(lambda p: pl.semaphore_signal(barrier, inc=1, device_id={"ctx": p}, device_id_type=MESH))
    over_replicas(lambda p: pl.semaphore_signal(barrier, inc=1, device_id={"dp": p}, device_id_type=MESH))

    def turn_filter(t, lanes):
        turned = long_filter[:, lanes].T
        filter_send[pl.ds(t * per_tile, per_tile)] = turned.reshape(per_tile, *filter_send.shape[1:])

    def turn_upstream(t, lanes):
        upstream_send[pl.ds(t * per_tile, per_tile)] = upstream_of(lanes).T.reshape(per_tile, *upstream_send.shape[1:])

    lane_tiles(turn_filter)
    lane_tiles(turn_upstream)
    pl.semaphore_wait(barrier, context - 1 + replicas - 1)

    push(keys_raw.at[0, pl.ds(tokens - 16, 16)], key_edge, 0, ctx=following)
    over_context(lambda p: push(filter_send.at[p, row], filter_seq.at[row, :, me], 1, ctx=p))
    keep(filter_send.at[me, row], filter_seq.at[row, :, me], 1)
    over_context(lambda p: push(upstream_send.at[p], upstream_seq.at[:, me], 2, ctx=p))
    keep(upstream_send.at[me], upstream_seq.at[:, me], 2)

    key_ext[pl.ds(8, tokens), :] = keys_raw[0].astype(jnp.float32)
    arrived(key_edge, 0)
    edge = key_edge[...].astype(jnp.float32)[8:]
    key_ext[pl.ds(0, 8), :] = jnp.where(me == 0, 0.0, edge)

    def make_gated(t, lanes):
        rows = (
            short_filter[0:1, lanes] * key_ext[pl.ds(8, tokens), lanes]
            + short_filter[1:2, lanes] * key_ext[pl.ds(7, tokens), lanes]
            + short_filter[2:3, lanes] * key_ext[pl.ds(6, tokens), lanes]
        )
        key_rows[:, lanes] = rows
        gated = rows * values[0, :, lanes].astype(jnp.float32)
        gated_send[pl.ds(t * per_tile, per_tile)] = gated.T.reshape(per_tile, *gated_send.shape[1:])

    lane_tiles(make_gated)
    over_context(lambda p: push(gated_send.at[p], gated_seq.at[:, me], 3, ctx=p))
    keep(gated_send.at[me], gated_seq.at[:, me], 3)

    arrived(filter_seq.at[row], 1)
    over_replicas(lambda p: push(filter_seq.at[row], filter_seq.at[row], 4, dp=p))

    arrived(upstream_seq, 2)
    forward(upstream_seq, upstream_freq, first, ahead, twist_cos, twist_sin)
    arrived(filter_seq.at[pl.ds(0, replicas - 1)], 4)
    filter_flat = filter_seq.reshape(upstream_seq.shape)
    forward(filter_flat, filter_freq, first, ahead, twist_cos, twist_sin)
    inverse(filter_freq, upstream_freq, True, back_seq, last, back, twist_cos, twist_sin)
    over_context(lambda p: push(back_seq.at[:, p], back_home.at[me], 5, ctx=p))
    keep(back_seq.at[:, me], back_home.at[me], 5)

    arrived(gated_seq, 3)
    forward(gated_seq, gated_freq, first, ahead, twist_cos, twist_sin)
    inverse(gated_freq, upstream_freq, True, lag_seq, last, back, twist_cos, twist_sin)
    lag_quarters = lag_seq.reshape(lag_parts.shape)
    over_replicas(lambda p: push(lag_quarters.at[p], lag_parts.at[row], 6, dp=p))
    keep(lag_quarters.at[row], lag_parts.at[row], 6)
    inverse(filter_freq, gated_freq, False, conv_seq, last, back, twist_cos, twist_sin)
    over_context(lambda p: push(conv_seq.at[:, p], conv_home.at[me], 7, ctx=p))
    keep(conv_seq.at[:, me], conv_home.at[me], 7)

    arrived(back_home, 5)

    def use_back(t, lanes):
        back_rows = back_home[pl.ds(t * per_tile, per_tile)].reshape(LANES, tokens).T
        upstream = upstream_of(lanes)
        grad_gated = back_rows + skip_gain[:, lanes] * upstream
        rows = key_rows[:, lanes]
        value_rows = values[0, :, lanes].astype(jnp.float32)
        grad_values[0, :, lanes] = (grad_gated * rows).astype(jnp.bfloat16)
        grad_rows = grad_gated * value_rows
        grad_key_ext[pl.ds(0, tokens), lanes] = grad_rows
        for j in range(3):
            terms[pl.ds(j * tiles + t, 1), :] = jnp.sum(
                grad_rows * key_ext[pl.ds(8 - j, tokens), lanes], axis=0, keepdims=True
            )
        terms[pl.ds(3 * tiles + t, 1), :] = jnp.sum(upstream * (rows * value_rows), axis=0, keepdims=True)

    lane_tiles(use_back)
    push(grad_key_ext.at[pl.ds(0, 8)], grad_key_ext.at[pl.ds(tokens, 8)], 8, ctx=preceding)
    over_context(lambda p: push(terms.at[pl.ds(p, 1)], terms_in.at[pl.ds(me, 1)], 9, ctx=p))
    keep(terms.at[pl.ds(me, 1)], terms_in.at[pl.ds(me, 1)], 9)

    arrived(lag_parts, 6)

    @pl.loop(0, lag_sum.shape[0])
    def _(c):
        total = lag_parts[0, c]
        for j in range(1, replicas):
            total = total + lag_parts[j, c]
        lag_sum[c] = total

    over_context(lambda p: push(lag_sum.at[:, p], lag_home.at[me, row], 10, ctx=p))
    keep(lag_sum.at[:, me], lag_home.at[me, row], 10)

    arrived(terms_in, 9)
    terms_dp[pl.ds(row, 1), :] = jnp.sum(terms_in[...], axis=0, keepdims=True)
    over_replicas(lambda p: push(terms_dp.at[pl.ds(row, 1)], terms_dp.at[pl.ds(row, 1)], 11, dp=p))

    arrived(grad_key_ext.at[pl.ds(tokens, 8)], 8)
    grad_key_ext[pl.ds(tokens, 8), :] = jnp.where(me == context - 1, 0.0, grad_key_ext[pl.ds(tokens, 8), :])

    def make_keys(t, lanes):
        grad_keys_raw[0, :, lanes] = (
            short_filter[0:1, lanes] * grad_key_ext[pl.ds(0, tokens), lanes]
            + short_filter[1:2, lanes] * grad_key_ext[pl.ds(1, tokens), lanes]
            + short_filter[2:3, lanes] * grad_key_ext[pl.ds(2, tokens), lanes]
        ).astype(jnp.bfloat16)

    lane_tiles(make_keys)

    arrived(terms_dp.at[pl.ds(0, replicas - 1)], 11)
    total = terms_dp[0:1, :]
    for j in range(1, replicas):
        total = total + terms_dp[j : j + 1, :]
    terms_all[pl.ds(me, 1), :] = total * grad_scale
    over_context(lambda p: push(terms_all.at[pl.ds(me, 1)], terms_all.at[pl.ds(me, 1)], 12, ctx=p))

    arrived(lag_home.at[:, row], 10)
    over_replicas(lambda p: push(lag_home.at[:, row], lag_home.at[:, row], 13, dp=p))

    arrived(conv_home, 7)

    def use_conv(t, lanes):
        conv_rows = conv_home[pl.ds(t * per_tile, per_tile)].reshape(LANES, tokens).T
        gated = key_rows[:, lanes] * values[0, :, lanes].astype(jnp.float32)
        grad_queries[0, :, lanes] = (
            grad_out[0, :, lanes].astype(jnp.float32) * (conv_rows + skip_gain[:, lanes] * gated)
        ).astype(jnp.bfloat16)

    lane_tiles(use_conv)

    arrived(lag_home.at[:, pl.ds(0, replicas - 1)], 13)

    def use_lag(t, lanes):
        turned = lag_home[pl.ds(t * per_tile, per_tile)].reshape(LANES, tokens).T
        grad_long[:, lanes] = turned * grad_scale

    lane_tiles(use_lag)

    arrived(terms_all.at[pl.ds(0, context - 1)], 12)
    for t in range(tiles):
        lanes = slice(t * LANES, (t + 1) * LANES)
        for j in range(3):
            grad_short[j : j + 1, lanes] = terms_all[j * tiles + t : j * tiles + t + 1, :]
        grad_skip[:, lanes] = terms_all[3 * tiles + t : 3 * tiles + t + 1, :]

    others = pl.ds(0, context - 1)
    peers = pl.ds(0, replicas - 1)
    sent(key_edge, 0)
    sent(filter_send.at[others, 0], 1)
    sent(upstream_send.at[others], 2)
    sent(gated_send.at[others], 3)
    sent(filter_seq.at[peers], 4)
    sent(back_home.at[others], 5)
    sent(lag_parts.at[peers], 6)
    sent(conv_home.at[others], 7)
    sent(grad_key_ext.at[pl.ds(tokens, 8)], 8)
    sent(terms.at[others], 9)
    sent(lag_home.at[others, 0], 10)
    sent(terms_dp.at[peers], 11)
    sent(terms_all.at[others], 12)
    sent(lag_home.at[:, peers], 13)


def per_device(context, replicas, queries, keys_raw, values, grad_out, short_filter, long_filter, skip_gain):
    _, tokens, width = queries.shape
    channels = width // context
    quarter = channels // replicas
    constants = [jnp.asarray(table) for table in tables(context, tokens)]
    grad_scale = 1.0 / math.sqrt(replicas * context * tokens)
    real = jnp.float32
    blocks = pltpu.VMEM((context, channels, tokens), real)
    sequences = pltpu.VMEM((channels, context, tokens), real)
    quarters = pltpu.VMEM((replicas, quarter, context, tokens), real)
    spectrum = pltpu.VMEM((channels * context, 2 * tokens), real)
    split_home = pltpu.VMEM((context, replicas, quarter, tokens), real)
    results = pl.pallas_call(
        functools.partial(kernel, context, replicas, grad_scale),
        out_shape=(
            jax.ShapeDtypeStruct(queries.shape, jnp.bfloat16),
            jax.ShapeDtypeStruct(queries.shape, jnp.bfloat16),
            jax.ShapeDtypeStruct(queries.shape, jnp.bfloat16),
            jax.ShapeDtypeStruct((tokens, width), real),
            jax.ShapeDtypeStruct((3, width), real),
            jax.ShapeDtypeStruct((1, width), real),
        ),
        in_specs=[pl.BlockSpec(memory_space=pltpu.VMEM)] * 13,
        out_specs=(pl.BlockSpec(memory_space=pltpu.VMEM),) * 6,
        scratch_shapes=[
            split_home,
            blocks,
            blocks,
            quarters,
            sequences,
            sequences,
            spectrum,
            spectrum,
            spectrum,
            sequences,
            sequences,
            sequences,
            blocks,
            blocks,
            quarters,
            pltpu.VMEM((quarter, context, tokens), real),
            split_home,
            pltpu.VMEM((16, width), jnp.bfloat16),
            pltpu.VMEM((tokens + 8, width), real),
            pltpu.VMEM((tokens, width), real),
            pltpu.VMEM((tokens + 8, width), real),
            pltpu.VMEM((context, LANES), real),
            pltpu.VMEM((context, LANES), real),
            pltpu.VMEM((8, LANES), real),
            pltpu.VMEM((context, LANES), real),
            pltpu.SemaphoreType.DMA((14,)),
            pltpu.SemaphoreType.DMA((14,)),
        ],
        compiler_params=pltpu.CompilerParams(
            collective_id=0, has_side_effects=True, vmem_limit_bytes=48 * 2**20
        ),
        name="long_convolution_backward",
    )(
        queries,
        keys_raw,
        values,
        grad_out,
        short_filter,
        long_filter,
        skip_gain.reshape(1, width),
        *constants,
    )
    grad_queries, grad_keys_raw, grad_values, grad_long, grad_short, grad_skip = results
    return grad_queries, grad_keys_raw, grad_values, grad_long, grad_short, grad_skip.reshape(width)


def solution(mesh):
    rows = P("dp", "ctx", "chan")
    return jax.shard_map(
        functools.partial(per_device, mesh.shape["ctx"], mesh.shape["dp"]),
        mesh=mesh,
        in_specs=(rows, rows, rows, rows, P(None, "chan"), P("ctx", "chan"), P("chan")),
        out_specs=(rows, rows, rows, P("ctx", "chan"), P(None, "chan"), P("chan")),
        check_vma=False,
    )
```

time: 977 us -> 89.1 us (0.09)
  blocking collectives: 663 us -> 0 us
  other arithmetic: 88.9 us -> 0 us
  local copies, waits for them, and re-layouts: 97 us -> 15.2 us
  Pallas kernels: 0 us -> 72.5 us
  starting transfers between devices: 54.7 us -> 0 us
  waiting for transfers between devices: 33.1 us -> 0 us
  matrix products: 19.9 us -> 0 us
  between operations: 15.4 us -> 0.67 us
    psum x1 -> x0, blocking collectives: 663 us -> none  [per_device(): short_total, skip_total = lax.psum((short_terms, skip_terms), ('dp', 'ctx'))]
    pallas_call x0 -> x1, Pallas kernels: none -> 72.5 us  [per_device(): pl.pallas_call(functools.partial(kernel, context, replicas, grad_scale),...]
    unnamed x3 -> x0, other arithmetic: 58.3 us -> none
    all_to_all x6 -> x0, starting transfers between devices: 40.9 us -> none  [the longest x1 10.3 us: per_device(): lax.all_to_all(filter_blocks, 'ctx', split_axis=0, concat_axis=2, tiled=T...]
    all_to_all x6 -> x0, waiting for transfers between devices: 25.9 us -> none  [the longest x1 15.6 us: per_device(): lax.all_to_all(gated_blocks, 'ctx', split_axis=0, concat_axis=2, tiled=True)]
    unnamed x106 -> x32, local copies, waits for them, and re-layouts: 39.1 us -> 15.2 us
    dot_general x6 -> x0, matrix products: 19.9 us -> none  [the longest x3 10.1 us: transform(): jnp.einsum('c...ab,cadk->d...kb', split, table, precision=lax.Precision.H...]
    squeeze x8 -> x0, local copies, waits for them, and re-layouts: 14.6 us -> none  [the longest x4 8.27 us: spectral(): mixed_real, mixed_imag = (mixed[0], mixed[1])]
  transfers between devices with their start and end apart: 9 -> 0, of which waited for: 4 -> 0; matrix products, arithmetic and copies ran while one was open for 10% -> 0% of each run, Pallas kernels for 0% -> 0%
where the time goes in v1:
time: 89.1 us; the launch traced here: 88.4 us
  Pallas kernels  72.5 us (81%)
  local copies, waits for them, and re-layouts  15.2 us (17%)
    pallas_call x1, Pallas kernels, per_device(): pl.pallas_call(functools.partial(kernel, context, replicas, grad_scale),...  72.5 us
    unnamed x32, local copies, waits for them, and re-layouts  15.2 us

profile of v1, /device:TPU:1, one launch (start us, length us, event | category | flops | bytes accessed | tf_op | source)
XLA Modules:
  0.0 88.4 jit_solution(2348227988744254981)
XLA Ops:
  0.6 0.0 copy-start
  0.6 1.0 %copy-done = f32[128,1024]{1,0:T(8,128)S(1)} copy-done((f32[128,1024]{1,0:T(8,128)S(1)}, f32[128,1024]{1,0:T(8,128)}, u32[]{:S(2)}) %copy-start) | copy-done | bytes 524312
  1.7 0.0 copy-start.1
  1.7 1.0 %copy-done.1 = bf16[768,256]{1,0:T(8,128)(2,1)S(1)} copy-done((bf16[768,256]{1,0:T(8,128)(2,1)S(1)}, bf16[768,256]{1,0:T(8,128)(2,1)}, u32[]{:S(2)}) %copy-start.1) | copy-done | bytes 393240
  2.7 0.0 copy-start.2
  2.7 1.0 %copy-done.2 = bf16[768,256]{1,0:T(8,128)(2,1)S(1)} copy-done((bf16[768,256]{1,0:T(8,128)(2,1)S(1)}, bf16[768,256]{1,0:T(8,128)(2,1)}, u32[]{:S(2)}) %copy-start.2) | copy-done | bytes 393240
  3.7 0.0 copy-start.3
  3.7 0.9 %copy-done.3 = bf16[1,128,1024]{2,1,0:T(8,128)(2,1)S(1)} copy-done((bf16[1,128,1024]{2,1,0:T(8,128)(2,1)S(1)}, bf16[1,128,1024]{2,1,0:T(8,128)(2,1)}, u32[]{:S(2)}) %copy-start.3) | copy-done | bytes 262168
  4.6 0.0 copy-start.4
  4.6 0.9 %copy-done.4 = bf16[1,128,1024]{2,1,0:T(8,128)(2,1)S(1)} copy-done((bf16[1,128,1024]{2,1,0:T(8,128)(2,1)S(1)}, bf16[1,128,1024]{2,1,0:T(8,128)(2,1)}, u32[]{:S(2)}) %copy-start.4) | copy-done | bytes 262168
  5.6 0.0 copy-start.5
  5.6 0.9 %copy-done.5 = bf16[1,128,1024]{2,1,0:T(8,128)(2,1)S(1)} copy-done((bf16[1,128,1024]{2,1,0:T(8,128)(2,1)S(1)}, bf16[1,128,1024]{2,1,0:T(8,128)(2,1)}, u32[]{:S(2)}) %copy-start.5) | copy-done | bytes 262168
  6.5 0.0 copy-start.6
  6.5 0.9 %copy-done.6 = bf16[1,128,1024]{2,1,0:T(8,128)(2,1)S(1)} copy-done((bf16[1,128,1024]{2,1,0:T(8,128)(2,1)S(1)}, bf16[1,128,1024]{2,1,0:T(8,128)(2,1)}, u32[]{:S(2)}) %copy-start.6) | copy-done | bytes 262168
  7.5 0.0 copy-start.7
  7.5 0.7 copy-done.7
  8.2 0.0 copy-start.8
  8.2 0.7 copy-done.8
  8.9 0.0 copy-start.9
  8.9 0.7 copy-done.9
  9.6 0.0 copy-start.10
  9.6 0.7 copy-done.10
  10.3 0.0 copy-start.11
  10.3 0.7 copy-done.11
  11.1 0.0 copy-start.12
  11.1 0.7 copy-done.12
  11.7 72.5 %long_convolution_backward.1 = (bf16[1,128,1024]{2,1,0:T(8,128)(2,1)S(1)}, bf16[1,128,1024]{2,1,0:T(8,128)(2,1)S(1)}, bf16[1,128,1024]{2,1,0:T(8,128)(2,1)S(1)},...) custom-call(bf16[1,128,1024]{2,1,0:T(8,128)(2,1)S(1)} %copy-done.3, ...), custom_call_target="tpu_custom_call" | custom-call | tf_op jit(solution)/shard_map/long_convolution_backward/pallas_call | solution.py:377
  84.3 0.7 copy.25
  85.0 0.7 copy.26
  85.7 0.7 copy.27
  86.4 0.8 copy.28
  87.2 0.6 copy.29
  87.8 0.6 copy.30
Async XLA Ops:
  0.6 1.0 %copy-start = (f32[128,1024]{1,0:T(8,128)S(1)}, f32[128,1024]{1,0:T(8,128)}, u32[]{:S(2)}) copy-start(f32[128,1024]{1,0:T(8,128)} %long_filter.1) | copy-start | bytes 1572868
  1.7 1.0 %copy-start.1 = (bf16[768,256]{1,0:T(8,128)(2,1)S(1)}, bf16[768,256]{1,0:T(8,128)(2,1)}, u32[]{:S(2)}) copy-start(bf16[768,256]{1,0:T(8,128)(2,1)} %constant.15.clone.back) | copy-start | bytes 1179652
  2.7 1.0 %copy-start.2 = (bf16[768,256]{1,0:T(8,128)(2,1)S(1)}, bf16[768,256]{1,0:T(8,128)(2,1)}, u32[]{:S(2)}) copy-start(bf16[768,256]{1,0:T(8,128)(2,1)} %constant.14.clone.ahead) | copy-start | bytes 1179652
  3.7 0.9 %copy-start.3 = (bf16[1,128,1024]{2,1,0:T(8,128)(2,1)S(1)}, bf16[1,128,1024]{2,1,0:T(8,128)(2,1)}, u32[]{:S(2)}) copy-start(bf16[1,128,1024]{2,1,0:T(8,128)(2,1)} %queries.1) | copy-start | bytes 786436
  4.6 0.9 %copy-start.4 = (bf16[1,128,1024]{2,1,0:T(8,128)(2,1)S(1)}, bf16[1,128,1024]{2,1,0:T(8,128)(2,1)}, u32[]{:S(2)}) copy-start(bf16[1,128,1024]{2,1,0:T(8,128)(2,1)} %keys_raw.1) | copy-start | bytes 786436
  5.6 0.9 %copy-start.5 = (bf16[1,128,1024]{2,1,0:T(8,128)(2,1)S(1)}, bf16[1,128,1024]{2,1,0:T(8,128)(2,1)}, u32[]{:S(2)}) copy-start(bf16[1,128,1024]{2,1,0:T(8,128)(2,1)} %values.1) | copy-start | bytes 786436
  6.5 0.9 %copy-start.6 = (bf16[1,128,1024]{2,1,0:T(8,128)(2,1)S(1)}, bf16[1,128,1024]{2,1,0:T(8,128)(2,1)}, u32[]{:S(2)}) copy-start(bf16[1,128,1024]{2,1,0:T(8,128)(2,1)} %grad_out.1) | copy-start | bytes 786436
  7.5 0.7 copy-start.7
  8.2 0.7 copy-start.8
  8.9 0.7 copy-start.9
  9.6 0.7 copy-start.10
  10.3 0.7 copy-start.11
  11.1 0.7 copy-start.12

commit v2 on v1

v2 whole, which is shorter than its diff:
```python
import functools
import math

import jax
import jax.numpy as jnp
import ml_dtypes
import numpy as np
from jax import lax
from jax.experimental import pallas as pl
from jax.experimental.pallas import tpu as pltpu
from jax.sharding import PartitionSpec as P

MESH = pl.DeviceIdType.MESH
LANES = 128
PACK = 8
ARGUMENTS = 13
POWER = 32
SHIFT = 125.0
STEPS = 230.0
SMALLEST = 1e-30


def two_parts(table):
    high = table.astype(ml_dtypes.bfloat16)
    low = (table - high.astype(np.float64)).astype(ml_dtypes.bfloat16)
    return high, low


def tables(blocks, tokens):
    full = blocks * tokens
    shifted = np.arange(blocks) + 0.25
    outer = 2.0 * np.pi * np.outer(shifted, np.arange(blocks)) / blocks
    first = np.concatenate([np.cos(outer), -np.sin(outer)], axis=0)
    last = np.concatenate([np.cos(outer).T, -np.sin(outer).T], axis=1) / full
    twist = 2.0 * np.pi * np.outer(shifted, np.arange(tokens)) / full
    inner = 2.0 * np.pi * np.outer(np.arange(tokens), np.arange(tokens)) / tokens
    cosine, sine = np.cos(inner), np.sin(inner)
    ahead = np.block([[cosine, -sine], [sine, cosine]])
    back = np.block([[cosine, sine], [-sine, cosine]])
    first_high, first_low = two_parts(first)
    last_high, last_low = two_parts(last)
    ahead_high, ahead_low = two_parts(ahead)
    back_high, back_low = two_parts(back)
    return (
        np.concatenate([first_high, first_high, first_low], axis=1),
        np.concatenate([last_high, last_high, last_low], axis=1),
        np.concatenate([ahead_high, ahead_high, ahead_low], axis=0),
        np.concatenate([back_high, back_high, back_low], axis=0),
        np.cos(twist).astype(np.float32),
        np.sin(twist).astype(np.float32),
    )


def encode(value, inverse_step):
    grown = (jnp.abs(value) * inverse_step + 1.0) * 2.0 ** (-SHIFT / POWER)
    for _ in range(POWER.bit_length() - 1):
        grown = grown * grown
    return jnp.where(value < 0.0, -grown, grown).astype(jnp.bfloat16)


def decode(code, step):
    code = code.astype(jnp.float32)
    grown = jnp.exp2((jnp.log2(jnp.abs(code)) + SHIFT) * (1.0 / POWER))
    value = grown * step - step
    return jnp.where(code < 0.0, -value, value)


def step_of(peak):
    top = jnp.max(jnp.max(peak, axis=0, keepdims=True), axis=1, keepdims=True)
    return jnp.broadcast_to(jnp.maximum(top, SMALLEST) * (1.0 / STEPS), (1, LANES))


def peak_of(value):
    rows = jnp.abs(value).reshape(-1, 8, value.shape[-1])
    rows = jnp.max(rows, axis=0)
    peak = rows[:, :LANES]
    for j in range(1, value.shape[-1] // LANES):
        peak = jnp.maximum(peak, rows[:, j * LANES : (j + 1) * LANES])
    return peak


def split_stack(value, axis):
    high = value.astype(jnp.bfloat16)
    low = (value - high.astype(jnp.float32)).astype(jnp.bfloat16)
    return jnp.concatenate([high, low, high], axis=axis)


def forward(source, target, first, ahead, twist_cos, twist_sin):
    channels, blocks, _ = source.shape

    @pl.loop(0, channels // PACK)
    def _(group):
        base = group * PACK
        rows = jnp.concatenate([source[base + j] for j in range(PACK)], axis=1)
        section = jnp.dot(first[...], split_stack(rows, 0), preferred_element_type=jnp.float32)
        cosine, sine = twist_cos[...], twist_sin[...]
        turned = []
        for j in range(PACK):
            real = section[:blocks, j * LANES : (j + 1) * LANES]
            imag = section[blocks:, j * LANES : (j + 1) * LANES]
            turned.append(jnp.concatenate([real * cosine + imag * sine, imag * cosine - real * sine], axis=1))
        turned = jnp.concatenate(turned, axis=0)
        size = PACK * blocks
        target[pl.ds(pl.multiple_of(group * size, size), size), :] = jnp.dot(
            split_stack(turned, 1), ahead[...], preferred_element_type=jnp.float32
        )


def inverse(left, right, conjugate, target, last, back, twist_cos, twist_sin):
    channels, blocks, _ = target.shape

    def work(group, peak):
        size = PACK * blocks
        rows = pl.ds(pl.multiple_of(group * size, size), size)
        a_real, a_imag = left[rows, :LANES], left[rows, LANES:]
        b_real, b_imag = right[rows, :LANES], right[rows, LANES:]
        if conjugate:
            real, imag = a_real * b_real + a_imag * b_imag, a_real * b_imag - a_imag * b_real
        else:
            real, imag = a_real * b_real - a_imag * b_imag, a_real * b_imag + a_imag * b_real
        product = jnp.concatenate([real, imag], axis=1)
        section = jnp.dot(split_stack(product, 1), back[...], preferred_element_type=jnp.float32)
        cosine, sine = twist_cos[...], twist_sin[...]
        turned = []
        for j in range(PACK):
            real = section[j * blocks : (j + 1) * blocks, :LANES]
            imag = section[j * blocks : (j + 1) * blocks, LANES:]
            turned.append(jnp.concatenate([real * cosine - imag * sine, real * sine + imag * cosine], axis=0))
        turned = jnp.concatenate(turned, axis=1)
        result = jnp.dot(last[...], split_stack(turned, 0), preferred_element_type=jnp.float32)
        for j in range(PACK):
            target[group * PACK + j] = result[:, j * LANES : (j + 1) * LANES]
        return jnp.maximum(peak, peak_of(result))

    return lax.fori_loop(0, channels // PACK, work, jnp.zeros((8, LANES), jnp.float32))


def kernel(
    context,
    replicas,
    grad_scale,
    *refs,
):
    given, refs = refs[:ARGUMENTS], refs[ARGUMENTS:]
    outcome, refs = refs[:6], refs[6:]
    held, refs = refs[:ARGUMENTS], refs[ARGUMENTS:]
    (grad_queries, grad_keys_raw, grad_values, grad_long, grad_short, grad_skip), refs = refs[:6], refs[6:]
    queries, keys_raw, values, grad_out, short_filter, long_filter, skip_gain, *constants = held
    first, last, ahead, back, twist_cos, twist_sin = constants
    (
        turned_rows,
        filter_code,
        upstream_code,
        gated_code,
        back_code,
        conv_code,
        lag_code,
        filter_in,
        upstream_in,
        gated_in,
        back_in,
        conv_in,
        lag_in,
        lag_home,
        lag_codes,
        filter_seq,
        upstream_seq,
        gated_seq,
        filter_freq,
        upstream_freq,
        gated_freq,
        back_seq,
        conv_seq,
        lag_seq,
        lag_sum,
        key_edge,
        key_ext,
        key_rows,
        grad_key_ext,
        terms,
        terms_in,
        terms_dp,
        terms_all,
        steps,
        filter_steps,
        upstream_steps,
        gated_steps,
        back_steps,
        conv_steps,
        lag_steps,
        home_steps,
        load_sem,
        store_sem,
        send_sem,
        recv_sem,
    ) = refs
    tokens, width = key_rows.shape
    channels = filter_seq.shape[0]
    quarter = channels // replicas
    me = lax.axis_index("ctx")
    row = lax.axis_index("dp")
    tiles = width // LANES
    per_tile = LANES // channels
    following = lax.rem(me + 1, context)
    preceding = lax.rem(me + context - 1, context)
    others = pl.ds(0, context - 1)
    peers = pl.ds(0, replicas - 1)

    def over_context(step):
        @pl.loop(1, context)
        def _(i):
            step(lax.rem(me + i, context))

    def over_replicas(step):
        @pl.loop(1, replicas)
        def _(i):
            step(lax.rem(row + i, replicas))

    def push(source, target, number, **peer):
        pltpu.make_async_remote_copy(
            src_ref=source,
            dst_ref=target,
            send_sem=send_sem.at[number],
            recv_sem=recv_sem.at[number],
            device_id=peer,
            device_id_type=MESH,
        ).start()

    def keep(source, target, number):
        pltpu.make_async_copy(source, target, recv_sem.at[number]).start()

    def arrived(extent, number):
        pltpu.make_async_copy(extent, extent, recv_sem.at[number]).wait()

    def sent(extent, number):
        pltpu.make_async_copy(extent, extent, send_sem.at[number]).wait()

    def lane_tiles(step):
        for t in range(tiles):
            step(t, slice(t * LANES, (t + 1) * LANES))

    def upstream_of(lanes):
        return grad_out[0, :, lanes].astype(jnp.float32) * queries[0, :, lanes].astype(jnp.float32)

    def hold_step(number, peak):
        step = step_of(peak)
        steps[number : number + 1, :] = step
        return 1.0 / step

    def code_rows(make, code, number):
        peak = jnp.zeros((8, LANES), jnp.float32)
        for t in range(tiles):
            part = make(slice(t * LANES, (t + 1) * LANES)).T
            turned_rows[t * per_tile : (t + 1) * per_tile] = part.reshape(per_tile, channels, tokens)
            peak = jnp.maximum(peak, peak_of(part))
        inverse_step = hold_step(number, peak)

        @pl.loop(0, context, unroll=4)
        def _(p):
            code[p] = encode(turned_rows[p], inverse_step)

    def code_sequences(sequences, code, number, peak):
        inverse_step = hold_step(number, peak)

        @pl.loop(0, context, unroll=4)
        def _(p):
            code[p] = encode(sequences[:, p], inverse_step)

    def open_sequences(code, found_steps, sequences):
        @pl.loop(0, context, unroll=4)
        def _(p):
            sequences[:, p] = decode(code[p], found_steps[pl.ds(p, 1), :])

    def exchange(code, code_in, step_number, steps_in, number):
        def one(p):
            push(code.at[p], code_in.at[me], number, ctx=p)
            push(steps.at[pl.ds(step_number, 1)], steps_in.at[pl.ds(me, 1)], number + 1, ctx=p)

        over_context(one)
        keep(code.at[me], code_in.at[me], number)
        keep(steps.at[pl.ds(step_number, 1)], steps_in.at[pl.ds(me, 1)], number + 1)

    def exchanged(code_in, steps_in, number):
        arrived(code_in, number)
        arrived(steps_in, number + 1)

    def store(i):
        made = (grad_queries, grad_keys_raw, grad_values, grad_long, grad_short, grad_skip)[i]
        return pltpu.make_async_copy(made, outcome[i], store_sem.at[i])

    def load(i):
        return pltpu.make_async_copy(given[i], held[i], load_sem.at[i])

    order = (5, 3, 0, 1, 2, 4, 6, 7, 9, 11, 12, 8, 10)
    for i in order:
        load(i).start()
    barrier = pltpu.get_barrier_semaphore()
    over_context(lambda p: pl.semaphore_signal(barrier, inc=1, device_id={"ctx": p}, device_id_type=MESH))
    over_replicas(lambda p: pl.semaphore_signal(barrier, inc=1, device_id={"dp": p}, device_id_type=MESH))

    load(5).wait()
    code_rows(lambda lanes: long_filter[:, lanes], filter_code, 0)
    load(3).wait()
    load(0).wait()
    code_rows(upstream_of, upstream_code, 1)
    pl.semaphore_wait(barrier, context - 1 + replicas - 1)

    push(given[1].at[0, pl.ds(tokens - 16, 16)], key_edge, 0, ctx=following)

    place, chosen = me // replicas, lax.rem(me, replicas) == row

    @pl.when(chosen)
    def _():
        def one(p):
            push(filter_code.at[p], filter_in.at[row, place], 1, ctx=p)
            push(steps.at[pl.ds(0, 1)], filter_steps.at[row, pl.ds(place, 1)], 2, ctx=p)

        over_context(one)
        keep(filter_code.at[me], filter_in.at[row, place], 1)
        keep(steps.at[pl.ds(0, 1)], filter_steps.at[row, pl.ds(place, 1)], 2)

    exchange(upstream_code, upstream_in, 1, upstream_steps, 5)

    load(1).wait()
    load(2).wait()
    load(4).wait()
    key_ext[pl.ds(8, tokens), :] = keys_raw[0].astype(jnp.float32)
    arrived(key_edge, 0)
    edge = key_edge[...].astype(jnp.float32)[8:]
    key_ext[pl.ds(0, 8), :] = jnp.where(me == 0, 0.0, edge)

    def gated_of(lanes):
        rows = (
            short_filter[0:1, lanes] * key_ext[pl.ds(8, tokens), lanes]
            + short_filter[1:2, lanes] * key_ext[pl.ds(7, tokens), lanes]
            + short_filter[2:3, lanes] * key_ext[pl.ds(6, tokens), lanes]
        )
        key_rows[:, lanes] = rows
        return rows * values[0, :, lanes].astype(jnp.float32)

    code_rows(gated_of, gated_code, 2)
    exchange(gated_code, gated_in, 2, gated_steps, 7)

    arrived(filter_in.at[row], 1)
    arrived(filter_steps.at[row], 2)

    def share_filter(p):
        push(filter_in.at[row], filter_in.at[row], 3, dp=p)
        push(filter_steps.at[row], filter_steps.at[row], 4, dp=p)

    over_replicas(share_filter)

    for i in range(6, ARGUMENTS):
        load(i).wait()
    exchanged(upstream_in, upstream_steps, 5)
    open_sequences(upstream_in, upstream_steps, upstream_seq)
    forward(upstream_seq, upstream_freq, first, ahead, twist_cos, twist_sin)
    arrived(filter_in.at[peers], 3)
    arrived(filter_steps.at[peers], 4)

    @pl.loop(0, context // replicas)
    def _(p):
        for q in range(replicas):
            filter_seq[:, p * replicas + q] = decode(filter_in[q, p], filter_steps[q, pl.ds(p, 1), :])

    forward(filter_seq, filter_freq, first, ahead, twist_cos, twist_sin)
    peak = inverse(filter_freq, upstream_freq, True, back_seq, last, back, twist_cos, twist_sin)
    code_sequences(back_seq, back_code, 3, peak)
    exchange(back_code, back_in, 3, back_steps, 9)

    exchanged(gated_in, gated_steps, 7)
    open_sequences(gated_in, gated_steps, gated_seq)
    forward(gated_seq, gated_freq, first, ahead, twist_cos, twist_sin)
    peak = inverse(gated_freq, upstream_freq, True, lag_seq, last, back, twist_cos, twist_sin)
    inverse_step = hold_step(4, peak)

    @pl.loop(0, channels, unroll=4)
    def _(c):
        lag_code[c // quarter, lax.rem(c, quarter)] = encode(lag_seq[c], inverse_step)

    def share_lag(p):
        push(lag_code.at[p], lag_in.at[row], 11, dp=p)
        push(steps.at[pl.ds(4, 1)], lag_steps.at[row], 12, dp=p)

    over_replicas(share_lag)
    keep(lag_code.at[row], lag_in.at[row], 11)
    keep(steps.at[pl.ds(4, 1)], lag_steps.at[row], 12)
    peak = inverse(filter_freq, gated_freq, False, conv_seq, last, back, twist_cos, twist_sin)
    code_sequences(conv_seq, conv_code, 5, peak)
    exchange(conv_code, conv_in, 5, conv_steps, 13)

    def home_rows(code_in, found_steps, t):
        parts = [decode(code_in[p], found_steps[p : p + 1, :]) for p in range(t * per_tile, (t + 1) * per_tile)]
        return jnp.concatenate(parts, axis=0).T

    exchanged(back_in, back_steps, 9)

    def use_back(t, lanes):
        back_rows = home_rows(back_in, back_steps, t)
        upstream = upstream_of(lanes)
        grad_gated = back_rows + skip_gain[:, lanes] * upstream
        rows = key_rows[:, lanes]
        value_rows = values[0, :, lanes].astype(jnp.float32)
        grad_values[0, :, lanes] = (grad_gated * rows).astype(jnp.bfloat16)
        grad_rows = grad_gated * value_rows
        grad_key_ext[pl.ds(0, tokens), lanes] = grad_rows
        for j in range(3):
            terms[j * tiles + t : j * tiles + t + 1, :] = jnp.sum(
                grad_rows * key_ext[pl.ds(8 - j, tokens), lanes], axis=0, keepdims=True
            )
        terms[3 * tiles + t : 3 * tiles + t + 1, :] = jnp.sum(upstream * (rows * value_rows), axis=0, keepdims=True)

    lane_tiles(use_back)
    push(grad_key_ext.at[pl.ds(0, 8)], grad_key_ext.at[pl.ds(tokens, 8)], 15, ctx=preceding)
    over_context(lambda p: push(terms.at[pl.ds(p, 1)], terms_in.at[pl.ds(me, 1)], 16, ctx=p))
    keep(terms.at[pl.ds(me, 1)], terms_in.at[pl.ds(me, 1)], 16)
    store(2).start()

    arrived(lag_in, 11)
    arrived(lag_steps, 12)

    @pl.loop(0, quarter)
    def _(c):
        total = decode(lag_in[0, c], lag_steps[0])
        for j in range(1, replicas):
            total = total + decode(lag_in[j, c], lag_steps[j])
        lag_sum[c] = total

    over_context(lambda p: push(lag_sum.at[:, p], lag_home.at[me], 17, ctx=p))
    keep(lag_sum.at[:, me], lag_home.at[me], 17)

    arrived(terms_in, 16)
    terms_dp[pl.ds(row, 1), :] = jnp.sum(terms_in[...], axis=0, keepdims=True)
    over_replicas(lambda p: push(terms_dp.at[pl.ds(row, 1)], terms_dp.at[pl.ds(row, 1)], 18, dp=p))

    arrived(grad_key_ext.at[pl.ds(tokens, 8)], 15)
    grad_key_ext[pl.ds(tokens, 8), :] = jnp.where(me == context - 1, 0.0, grad_key_ext[pl.ds(tokens, 8), :])

    def make_keys(t, lanes):
        grad_keys_raw[0, :, lanes] = (
            short_filter[0:1, lanes] * grad_key_ext[pl.ds(0, tokens), lanes]
            + short_filter[1:2, lanes] * grad_key_ext[pl.ds(1, tokens), lanes]
            + short_filter[2:3, lanes] * grad_key_ext[pl.ds(2, tokens), lanes]
        ).astype(jnp.bfloat16)

    lane_tiles(make_keys)
    store(1).start()

    arrived(terms_dp.at[peers], 18)
    total = terms_dp[0:1, :]
    for j in range(1, replicas):
        total = total + terms_dp[j : j + 1, :]
    terms_all[pl.ds(me, 1), :] = total * grad_scale
    over_context(lambda p: push(terms_all.at[pl.ds(me, 1)], terms_all.at[pl.ds(me, 1)], 19, ctx=p))

    arrived(lag_home, 17)
    home = lag_home[...].reshape(context * quarter, tokens)
    inverse_step = hold_step(6, peak_of(home))
    lag_codes[row] = encode(home, inverse_step)
    home_steps[row] = steps[6:7, :]

    def share_home(p):
        push(lag_codes.at[row], lag_codes.at[row], 20, dp=p)
        push(home_steps.at[row], home_steps.at[row], 21, dp=p)

    over_replicas(share_home)

    exchanged(conv_in, conv_steps, 13)

    def use_conv(t, lanes):
        conv_rows = home_rows(conv_in, conv_steps, t)
        gated = key_rows[:, lanes] * values[0, :, lanes].astype(jnp.float32)
        grad_queries[0, :, lanes] = (
            grad_out[0, :, lanes].astype(jnp.float32) * (conv_rows + skip_gain[:, lanes] * gated)
        ).astype(jnp.bfloat16)

    lane_tiles(use_conv)
    store(0).start()

    arrived(lag_codes.at[peers], 20)
    arrived(home_steps.at[peers], 21)

    def use_lag(t, lanes):
        size = per_tile * quarter
        parts = [decode(lag_codes[q, t * size : (t + 1) * size, :], home_steps[q]) for q in range(replicas)]
        rows = [parts[q][p * quarter : (p + 1) * quarter] for p in range(per_tile) for q in range(replicas)]
        grad_long[:, lanes] = jnp.concatenate(rows, axis=0).T * grad_scale

    lane_tiles(use_lag)
    store(3).start()

    arrived(terms_all.at[others], 19)
    for t in range(tiles):
        lanes = slice(t * LANES, (t + 1) * LANES)
        for j in range(3):
            grad_short[j : j + 1, lanes] = terms_all[j * tiles + t : j * tiles + t + 1, :]
        grad_skip[:, lanes] = terms_all[3 * tiles + t : 3 * tiles + t + 1, :]
    store(4).start()
    store(5).start()
    for i in range(6):
        store(i).wait()

    sent(key_edge, 0)

    @pl.when(chosen)
    def _():
        sent(filter_code.at[others], 1)
        sent(upstream_steps.at[others], 2)

    sent(filter_in.at[peers], 3)
    sent(filter_steps.at[peers], 4)
    for number in (5, 7, 9, 13):
        sent(upstream_in.at[others], number)
        sent(upstream_steps.at[others], number + 1)
    sent(lag_code.at[peers], 11)
    sent(lag_steps.at[peers], 12)
    sent(grad_key_ext.at[pl.ds(tokens, 8)], 15)
    sent(terms.at[others], 16)
    sent(lag_home.at[others], 17)
    sent(terms_dp.at[peers], 18)
    sent(terms_all.at[others], 19)
    sent(lag_codes.at[peers], 20)
    sent(home_steps.at[peers], 21)


def settle(*refs):
    count = (len(refs) - 2) // 3
    given, made, held = refs[:count], refs[count : 2 * count], refs[2 * count : 3 * count]
    loads = [pltpu.make_async_copy(given[i], held[i], refs[-2].at[i]) for i in range(count)]
    stores = [pltpu.make_async_copy(held[i], made[i], refs[-1].at[i]) for i in range(count)]
    for copy in loads:
        copy.start()
    for load, store in zip(loads, stores):
        load.wait()
        store.start()
    for copy in stores:
        copy.wait()


def per_device(context, replicas, queries, keys_raw, values, grad_out, short_filter, long_filter, skip_gain):
    _, tokens, width = queries.shape
    channels = width // context
    quarter = channels // replicas
    constants = [jnp.asarray(table) for table in tables(context, tokens)]
    grad_scale = 1.0 / math.sqrt(replicas * context * tokens)
    real = jnp.float32
    half = jnp.bfloat16
    coded = pltpu.VMEM((context, channels, tokens), half)
    sequences = pltpu.VMEM((channels, context, tokens), real)
    spectrum = pltpu.VMEM((channels * context, 2 * tokens), real)
    by_position = pltpu.VMEM((context, LANES), real)
    outputs = (
        jax.ShapeDtypeStruct(queries.shape, jnp.bfloat16),
        jax.ShapeDtypeStruct(queries.shape, jnp.bfloat16),
        jax.ShapeDtypeStruct(queries.shape, jnp.bfloat16),
        jax.ShapeDtypeStruct((tokens, width), real),
        jax.ShapeDtypeStruct((3, width), real),
        jax.ShapeDtypeStruct((1, width), real),
    )
    arguments = (queries, keys_raw, values, grad_out, short_filter, long_filter, skip_gain.reshape(1, width), *constants)
    results = pl.pallas_call(
        functools.partial(kernel, context, replicas, grad_scale),
        out_shape=outputs,
        in_specs=[pl.BlockSpec(memory_space=pltpu.HBM)] * ARGUMENTS,
        out_specs=(pl.BlockSpec(memory_space=pltpu.HBM),) * 6,
        scratch_shapes=[
            *(pltpu.VMEM(argument.shape, argument.dtype) for argument in arguments),
            *(pltpu.VMEM(output.shape, output.dtype) for output in outputs),
            pltpu.VMEM((context, channels, tokens), real),
            *(coded,) * 5,
            pltpu.VMEM((replicas, quarter, context, tokens), half),
            pltpu.VMEM((replicas, context // replicas, channels, tokens), half),
            *(coded,) * 4,
            pltpu.VMEM((replicas, quarter, context, tokens), half),
            pltpu.VMEM((context, quarter, tokens), real),
            pltpu.VMEM((replicas, context * quarter, tokens), half),
            *(sequences,) * 3,
            *(spectrum,) * 3,
            *(sequences,) * 3,
            pltpu.VMEM((quarter, context, tokens), real),
            pltpu.VMEM((16, width), half),
            pltpu.VMEM((tokens + 8, width), real),
            pltpu.VMEM((tokens, width), real),
            pltpu.VMEM((tokens + 8, width), real),
            *(by_position,) * 2,
            pltpu.VMEM((8, LANES), real),
            by_position,
            pltpu.VMEM((8, LANES), real),
            pltpu.VMEM((replicas, context // replicas, LANES), real),
            *(by_position,) * 4,
            *(pltpu.VMEM((replicas, 1, LANES), real),) * 2,
            pltpu.SemaphoreType.DMA((ARGUMENTS,)),
            pltpu.SemaphoreType.DMA((6,)),
            pltpu.SemaphoreType.DMA((22,)),
            pltpu.SemaphoreType.DMA((22,)),
        ],
        compiler_params=pltpu.CompilerParams(
            collective_id=0, has_side_effects=True, vmem_limit_bytes=63 * 2**20
        ),
        name="long_convolution_backward",
    )(*arguments)
    results = pl.pallas_call(
        settle,
        out_shape=outputs,
        in_specs=[pl.BlockSpec(memory_space=pltpu.HBM)] * len(results),
        out_specs=(pl.BlockSpec(memory_space=pltpu.HBM),) * len(results),
        scratch_shapes=[
            *(pltpu.VMEM(result.shape, result.dtype) for result in results),
            pltpu.SemaphoreType.DMA((len(results),)),
            pltpu.SemaphoreType.DMA((len(results),)),
        ],
        compiler_params=pltpu.CompilerParams(vmem_limit_bytes=63 * 2**20),
        name="settle",
    )(*results)
    grad_queries, grad_keys_raw, grad_values, grad_long, grad_short, grad_skip = results
    return grad_queries, grad_keys_raw, grad_values, grad_long, grad_short, grad_skip.reshape(width)


def solution(mesh):
    rows = P("dp", "ctx", "chan")
    return jax.shard_map(
        functools.partial(per_device, mesh.shape["ctx"], mesh.shape["dp"]),
        mesh=mesh,
        in_specs=(rows, rows, rows, rows, P(None, "chan"), P("ctx", "chan"), P("chan")),
        out_specs=(rows, rows, rows, P("ctx", "chan"), P(None, "chan"), P("chan")),
        check_vma=False,
    )
```

time: 89.1 us -> 66.9 us (0.75)
  local copies, waits for them, and re-layouts: 15.2 us -> 0 us
  Pallas kernels: 72.5 us -> 66.1 us
    unnamed x32 -> x0, local copies, waits for them, and re-layouts: 15.2 us -> none
    pallas_call x1, Pallas kernels: 72.5 us -> 63.9 us  [per_device(): pl.pallas_call(functools.partial(kernel, context, replicas, grad_scale),...]
    pallas_call x0 -> x1, Pallas kernels: none -> 2.18 us  [per_device(): pl.pallas_call(settle, out_shape=outputs, in_specs=[pl.BlockSpec(memory_s...]
where the time goes in v2:
time: 66.9 us; the launch traced here: 66.7 us
  Pallas kernels  66.1 us (99%)
    pallas_call x1, Pallas kernels, per_device(): pl.pallas_call(functools.partial(kernel, context, replicas, grad_scale),...  63.9 us
    pallas_call x1, Pallas kernels, per_device(): pl.pallas_call(settle, out_shape=outputs, in_specs=[pl.BlockSpec(memory_s...  2.18 us

profile of v2, /device:TPU:1, one launch (start us, length us, event | category | flops | bytes accessed | tf_op | source)
XLA Modules:
  0.0 66.7 jit_solution(4426483947349386848)
XLA Ops:
  0.6 63.9 %long_convolution_backward.1 = (bf16[1,128,1024]{2,1,0:T(8,128)(2,1)}, bf16[1,128,1024]{2,1,0:T(8,128)(2,1)}, bf16[1,128,1024]{2,1,0:T(8,128)(2,1)}, f32[128,102...) custom-call(bf16[1,128,1024]{2,1,0:T(8,128)(2,1)} %refs_0_.1, bf16[1,128,1024]{2,1,0:T(8,128)(2,1)} %refs_1_.1, ...), custom_call_target="tpu_custom_call" | custom-call | tf_op jit(solution)/shard_map/long_convolution_backward/pallas_call | solution.py:561
  64.6 2.2 %settle.1 = (bf16[1,128,1024]{2,1,0:T(8,128)(2,1)}, bf16[1,128,1024]{2,1,0:T(8,128)(2,1)}, bf16[1,128,1024]{2,1,0:T(8,128)(2,1)}, f32[128,1024]{1,0:T(8,128)}, f32[3,1024]{1,0:T(4,128)}, /*index=5*/f32[1,1024]{1,0:T(1,128)}) custom-call(bf16[1,128,1024]{2,1,0:T(8,128)(2,1)} %get-tuple-element.18.refs_0_, bf16[1,128,1024]{2,1,0:T(8,128)(2,1)} %get-tuple-element.19.refs_1_, ...), custom_call_target="tpu_custom_call" | custom-call | tf_op jit(solution)/shard_map/settle/pallas_call | solution.py:602

commit v3 on v2

--- a/solution.py
+++ b/solution.py
@@ -12,12 +12,13 @@
 
 MESH = pl.DeviceIdType.MESH
 LANES = 128
-PACK = 8
+PACK = 16
 ARGUMENTS = 13
 POWER = 32
 SHIFT = 125.0
 STEPS = 230.0
 SMALLEST = 1e-30
+EARLY = 16
 
 
 def two_parts(table):
@@ -88,8 +89,7 @@
 def forward(source, target, first, ahead, twist_cos, twist_sin):
     channels, blocks, _ = source.shape
 
-    @pl.loop(0, channels // PACK)
-    def _(group):
+    for group in range(channels // PACK):
         base = group * PACK
         rows = jnp.concatenate([source[base + j] for j in range(PACK)], axis=1)
         section = jnp.dot(first[...], split_stack(rows, 0), preferred_element_type=jnp.float32)
@@ -101,17 +101,18 @@
             turned.append(jnp.concatenate([real * cosine + imag * sine, imag * cosine - real * sine], axis=1))
         turned = jnp.concatenate(turned, axis=0)
         size = PACK * blocks
-        target[pl.ds(pl.multiple_of(group * size, size), size), :] = jnp.dot(
+        target[group * size : (group + 1) * size, :] = jnp.dot(
             split_stack(turned, 1), ahead[...], preferred_element_type=jnp.float32
         )
 
 
 def inverse(left, right, conjugate, target, last, back, twist_cos, twist_sin):
-    channels, blocks, _ = target.shape
-
-    def work(group, peak):
+    blocks, channels, _ = target.shape
+
+    peak = jnp.zeros((8, LANES), jnp.float32)
+    for group in range(channels // PACK):
         size = PACK * blocks
-        rows = pl.ds(pl.multiple_of(group * size, size), size)
+        rows = slice(group * size, (group + 1) * size)
         a_real, a_imag = left[rows, :LANES], left[rows, LANES:]
         b_real, b_imag = right[rows, :LANES], right[rows, LANES:]
         if conjugate:
@@ -129,10 +130,9 @@
         turned = jnp.concatenate(turned, axis=1)
         result = jnp.dot(last[...], split_stack(turned, 0), preferred_element_type=jnp.float32)
         for j in range(PACK):
-            target[group * PACK + j] = result[:, j * LANES : (j + 1) * LANES]
-        return jnp.maximum(peak, peak_of(result))
-
-    return lax.fori_loop(0, channels // PACK, work, jnp.zeros((8, LANES), jnp.float32))
+            target[:, group * PACK + j, :] = result[:, j * LANES : (j + 1) * LANES]
+        peak = jnp.maximum(peak, peak_of(result))
+    return peak
 
 
 def kernel(
@@ -162,7 +162,7 @@
         conv_in,
         lag_in,
         lag_home,
-        lag_codes,
+        lag_sum_code,
         filter_seq,
         upstream_seq,
         gated_seq,
@@ -196,7 +196,6 @@
     ) = refs
     tokens, width = key_rows.shape
     channels = filter_seq.shape[0]
-    quarter = channels // replicas
     me = lax.axis_index("ctx")
     row = lax.axis_index("dp")
     tiles = width // LANES
@@ -206,8 +205,8 @@
     others = pl.ds(0, context - 1)
     peers = pl.ds(0, replicas - 1)
 
-    def over_context(step):
-        @pl.loop(1, context)
+    def over_context(step, start=1, stop=context):
+        @pl.loop(start, stop)
         def _(i):
             step(lax.rem(me + i, context))
 
@@ -255,30 +254,28 @@
             peak = jnp.maximum(peak, peak_of(part))
         inverse_step = hold_step(number, peak)
 
-        @pl.loop(0, context, unroll=4)
-        def _(p):
+        for p in range(context):
             code[p] = encode(turned_rows[p], inverse_step)
 
     def code_sequences(sequences, code, number, peak):
         inverse_step = hold_step(number, peak)
 
-        @pl.loop(0, context, unroll=4)
-        def _(p):
-            code[p] = encode(sequences[:, p], inverse_step)
+        for p in range(context):
+            code[p] = encode(sequences[p], inverse_step)
 
     def open_sequences(code, found_steps, sequences):
-        @pl.loop(0, context, unroll=4)
-        def _(p):
-            sequences[:, p] = decode(code[p], found_steps[pl.ds(p, 1), :])
-
-    def exchange(code, code_in, step_number, steps_in, number):
+        for p in range(context):
+            sequences[:, p] = decode(code[p], found_steps[p : p + 1, :])
+
+    def exchange(code, code_in, step_number, steps_in, number, start=1, stop=context):
         def one(p):
             push(code.at[p], code_in.at[me], number, ctx=p)
             push(steps.at[pl.ds(step_number, 1)], steps_in.at[pl.ds(me, 1)], number + 1, ctx=p)
 
-        over_context(one)
-        keep(code.at[me], code_in.at[me], number)
-        keep(steps.at[pl.ds(step_number, 1)], steps_in.at[pl.ds(me, 1)], number + 1)
+        over_context(one, start, stop)
+        if start == 1:
+            keep(code.at[me], code_in.at[me], number)
+            keep(steps.at[pl.ds(step_number, 1)], steps_in.at[pl.ds(me, 1)], number + 1)
 
     def exchanged(code_in, steps_in, number):
         arrived(code_in, number)
@@ -307,17 +304,24 @@
 
     push(given[1].at[0, pl.ds(tokens - 16, 16)], key_edge, 0, ctx=following)
 
-    place, chosen = me // replicas, lax.rem(me, replicas) == row
-
-    @pl.when(chosen)
-    def _():
-        def one(p):
-            push(filter_code.at[p], filter_in.at[row, place], 1, ctx=p)
-            push(steps.at[pl.ds(0, 1)], filter_steps.at[row, pl.ds(place, 1)], 2, ctx=p)
-
-        over_context(one)
-        keep(filter_code.at[me], filter_in.at[row, place], 1)
-        keep(steps.at[pl.ds(0, 1)], filter_steps.at[row, pl.ds(place, 1)], 2)
+    place = me // replicas
+    sender_class = lax.rem(me, replicas)
+    taken = lax.rem(row + context - sender_class, replicas)
+    own_block = taken == sender_class
+
+    @pl.loop(0, context // replicas)
+    def _(i):
+        p = taken + i * replicas
+
+        @pl.when(p != me)
+        def _():
+            push(filter_code.at[p], filter_in.at[sender_class, place], 1, ctx=p)
+            push(steps.at[pl.ds(0, 1)], filter_steps.at[sender_class, pl.ds(place, 1)], 2, ctx=p)
+
+        @pl.when(p == me)
+        def _():
+            keep(filter_code.at[me], filter_in.at[sender_class, place], 1)
+            keep(steps.at[pl.ds(0, 1)], filter_steps.at[sender_class, pl.ds(place, 1)], 2)
 
     exchange(upstream_code, upstream_in, 1, upstream_steps, 5)
 
@@ -340,30 +344,27 @@
 
     code_rows(gated_of, gated_code, 2)
     exchange(gated_code, gated_in, 2, gated_steps, 7)
-
-    arrived(filter_in.at[row], 1)
-    arrived(filter_steps.at[row], 2)
+    arrived(filter_in.at[taken], 1)
+    arrived(filter_steps.at[taken], 2)
 
     def share_filter(p):
-        push(filter_in.at[row], filter_in.at[row], 3, dp=p)
-        push(filter_steps.at[row], filter_steps.at[row], 4, dp=p)
+        push(filter_in.at[taken], filter_in.at[taken], 3, dp=p)
+        push(filter_steps.at[taken], filter_steps.at[taken], 4, dp=p)
 
     over_replicas(share_filter)
 
     for i in range(6, ARGUMENTS):
         load(i).wait()
+    arrived(filter_in.at[peers], 3)
+    arrived(filter_steps.at[peers], 4)
+    for p in range(context):
+        sender, part = p % replicas, p // replicas
+        filter_seq[:, p] = decode(filter_in[sender, part], filter_steps[sender, part : part + 1, :])
+
+    forward(filter_seq, filter_freq, first, ahead, twist_cos, twist_sin)
     exchanged(upstream_in, upstream_steps, 5)
     open_sequences(upstream_in, upstream_steps, upstream_seq)
     forward(upstream_seq, upstream_freq, first, ahead, twist_cos, twist_sin)
-    arrived(filter_in.at[peers], 3)
-    arrived(filter_steps.at[peers], 4)
-
-    @pl.loop(0, context // replicas)
-    def _(p):
-        for q in range(replicas):
-            filter_seq[:, p * replicas + q] = decode(filter_in[q, p], filter_steps[q, pl.ds(p, 1), :])
-
-    forward(filter_seq, filter_freq, first, ahead, twist_cos, twist_sin)
     peak = inverse(filter_freq, upstream_freq, True, back_seq, last, back, twist_cos, twist_sin)
     code_sequences(back_seq, back_code, 3, peak)
     exchange(back_code, back_in, 3, back_steps, 9)
@@ -374,24 +375,52 @@
     peak = inverse(gated_freq, upstream_freq, True, lag_seq, last, back, twist_cos, twist_sin)
     inverse_step = hold_step(4, peak)
 
-    @pl.loop(0, channels, unroll=4)
-    def _(c):
-        lag_code[c // quarter, lax.rem(c, quarter)] = encode(lag_seq[c], inverse_step)
+    for part in range(context // replicas):
+        for c in range(replicas):
+            lag_code[c, part] = encode(lag_seq[part * replicas + c], inverse_step)
 
     def share_lag(p):
-        push(lag_code.at[p], lag_in.at[row], 11, dp=p)
+        push(lag_code.at[lax.rem(p + context - sender_class, replicas)], lag_in.at[row], 11, dp=p)
         push(steps.at[pl.ds(4, 1)], lag_steps.at[row], 12, dp=p)
 
     over_replicas(share_lag)
-    keep(lag_code.at[row], lag_in.at[row], 11)
+    keep(lag_code.at[taken], lag_in.at[row], 11)
     keep(steps.at[pl.ds(4, 1)], lag_steps.at[row], 12)
     peak = inverse(filter_freq, gated_freq, False, conv_seq, last, back, twist_cos, twist_sin)
     code_sequences(conv_seq, conv_code, 5, peak)
-    exchange(conv_code, conv_in, 5, conv_steps, 13)
+    exchange(conv_code, conv_in, 5, conv_steps, 13, stop=EARLY)
 
     def home_rows(code_in, found_steps, t):
         parts = [decode(code_in[p], found_steps[p : p + 1, :]) for p in range(t * per_tile, (t + 1) * per_tile)]
         return jnp.concatenate(parts, axis=0).T
+
+    arrived(lag_in, 11)
+    arrived(lag_steps, 12)
+
+    peak = jnp.zeros((8, LANES), jnp.float32)
+    for part in range(context // replicas):
+        total = decode(lag_in[0, part], lag_steps[0])
+        for j in range(1, replicas):
+            total = total + decode(lag_in[j, part], lag_steps[j])
+        lag_sum[part] = total
+        peak = jnp.maximum(peak, peak_of(total))
+    inverse_step = hold_step(6, peak)
+    for part in range(context // replicas):
+        lag_sum_code[part] = encode(lag_sum[part], inverse_step)
+
+    @pl.loop(0, context // replicas)
+    def _(i):
+        p = taken + i * replicas
+
+        @pl.when(p != me)
+        def _():
+            push(lag_sum_code.at[i], lag_home.at[sender_class, place], 17, ctx=p)
+            push(steps.at[pl.ds(6, 1)], home_steps.at[sender_class, pl.ds(place, 1)], 18, ctx=p)
+
+        @pl.when(p == me)
+        def _():
+            keep(lag_sum_code.at[i], lag_home.at[sender_class, place], 17)
+            keep(steps.at[pl.ds(6, 1)], home_steps.at[sender_class, pl.ds(place, 1)], 18)
 
     exchanged(back_in, back_steps, 9)
 
@@ -416,22 +445,20 @@
     keep(terms.at[pl.ds(me, 1)], terms_in.at[pl.ds(me, 1)], 16)
     store(2).start()
 
-    arrived(lag_in, 11)
-    arrived(lag_steps, 12)
-
-    @pl.loop(0, quarter)
-    def _(c):
-        total = decode(lag_in[0, c], lag_steps[0])
-        for j in range(1, replicas):
-            total = total + decode(lag_in[j, c], lag_steps[j])
-        lag_sum[c] = total
-
-    over_context(lambda p: push(lag_sum.at[:, p], lag_home.at[me], 17, ctx=p))
-    keep(lag_sum.at[:, me], lag_home.at[me], 17)
+    exchange(conv_code, conv_in, 5, conv_steps, 13, start=EARLY)
+
+    arrived(lag_home.at[taken], 17)
+    arrived(home_steps.at[taken], 18)
+
+    def share_home(p):
+        push(lag_home.at[taken], lag_home.at[taken], 20, dp=p)
+        push(home_steps.at[taken], home_steps.at[taken], 21, dp=p)
+
+    over_replicas(share_home)
 
     arrived(terms_in, 16)
     terms_dp[pl.ds(row, 1), :] = jnp.sum(terms_in[...], axis=0, keepdims=True)
-    over_replicas(lambda p: push(terms_dp.at[pl.ds(row, 1)], terms_dp.at[pl.ds(row, 1)], 18, dp=p))
+    over_replicas(lambda p: push(terms_dp.at[pl.ds(row, 1)], terms_dp.at[pl.ds(row, 1)], 22, dp=p))
 
     arrived(grad_key_ext.at[pl.ds(tokens, 8)], 15)
     grad_key_ext[pl.ds(tokens, 8), :] = jnp.where(me == context - 1, 0.0, grad_key_ext[pl.ds(tokens, 8), :])
@@ -446,24 +473,25 @@
     lane_tiles(make_keys)
     store(1).start()
 
-    arrived(terms_dp.at[peers], 18)
+    arrived(terms_dp.at[peers], 22)
     total = terms_dp[0:1, :]
     for j in range(1, replicas):
         total = total + terms_dp[j : j + 1, :]
     terms_all[pl.ds(me, 1), :] = total * grad_scale
     over_context(lambda p: push(terms_all.at[pl.ds(me, 1)], terms_all.at[pl.ds(me, 1)], 19, ctx=p))
 
-    arrived(lag_home, 17)
-    home = lag_home[...].reshape(context * quarter, tokens)
-    inverse_step = hold_step(6, peak_of(home))
-    lag_codes[row] = encode(home, inverse_step)
-    home_steps[row] = steps[6:7, :]
-
-    def share_home(p):
-        push(lag_codes.at[row], lag_codes.at[row], 20, dp=p)
-        push(home_steps.at[row], home_steps.at[row], 21, dp=p)
-
-    over_replicas(share_home)
+    arrived(lag_home.at[peers], 20)
+    arrived(home_steps.at[peers], 21)
+
+    def use_lag(t, lanes):
+        parts = []
+        for p in range(t * per_tile, (t + 1) * per_tile):
+            sender, part = p % replicas, p // replicas
+            parts.append(decode(lag_home[sender, part], home_steps[sender, part : part + 1, :]))
+        grad_long[:, lanes] = jnp.concatenate(parts, axis=0).T * grad_scale
+
+    lane_tiles(use_lag)
+    store(3).start()
 
     exchanged(conv_in, conv_steps, 13)
 
@@ -476,18 +504,6 @@
 
     lane_tiles(use_conv)
     store(0).start()
-
-    arrived(lag_codes.at[peers], 20)
-    arrived(home_steps.at[peers], 21)
-
-    def use_lag(t, lanes):
-        size = per_tile * quarter
-        parts = [decode(lag_codes[q, t * size : (t + 1) * size, :], home_steps[q]) for q in range(replicas)]
-        rows = [parts[q][p * quarter : (p + 1) * quarter] for p in range(per_tile) for q in range(replicas)]
-        grad_long[:, lanes] = jnp.concatenate(rows, axis=0).T * grad_scale
-
-    lane_tiles(use_lag)
-    store(3).start()
 
     arrived(terms_all.at[others], 19)
     for t in range(tiles):
@@ -502,10 +518,20 @@
 
     sent(key_edge, 0)
 
-    @pl.when(chosen)
+    @pl.when(own_block)
     def _():
-        sent(filter_code.at[others], 1)
-        sent(upstream_steps.at[others], 2)
+        extent = pl.ds(0, context // replicas - 1)
+        sent(filter_in.at[0, extent], 1)
+        sent(filter_steps.at[0, extent], 2)
+        sent(filter_in.at[0, extent], 17)
+        sent(filter_steps.at[0, extent], 18)
+
+    @pl.when(jnp.logical_not(own_block))
+    def _():
+        sent(filter_in.at[0], 1)
+        sent(filter_steps.at[0], 2)
+        sent(filter_in.at[0], 17)
+        sent(filter_steps.at[0], 18)
 
     sent(filter_in.at[peers], 3)
     sent(filter_steps.at[peers], 4)
@@ -516,10 +542,9 @@
     sent(lag_steps.at[peers], 12)
     sent(grad_key_ext.at[pl.ds(tokens, 8)], 15)
     sent(terms.at[others], 16)
-    sent(lag_home.at[others], 17)
-    sent(terms_dp.at[peers], 18)
+    sent(terms_dp.at[peers], 22)
     sent(terms_all.at[others], 19)
-    sent(lag_codes.at[peers], 20)
+    sent(lag_home.at[peers], 20)
     sent(home_steps.at[peers], 21)
 
 
@@ -540,11 +565,12 @@
 def per_device(context, replicas, queries, keys_raw, values, grad_out, short_filter, long_filter, skip_gain):
     _, tokens, width = queries.shape
     channels = width // context
-    quarter = channels // replicas
+    share = context // replicas
     constants = [jnp.asarray(table) for table in tables(context, tokens)]
     grad_scale = 1.0 / math.sqrt(replicas * context * tokens)
     real = jnp.float32
     half = jnp.bfloat16
+    by_class = pltpu.VMEM((replicas, share, channels, tokens), half)
     coded = pltpu.VMEM((context, channels, tokens), half)
     sequences = pltpu.VMEM((channels, context, tokens), real)
     spectrum = pltpu.VMEM((channels * context, 2 * tokens), real)
@@ -568,16 +594,15 @@
             *(pltpu.VMEM(output.shape, output.dtype) for output in outputs),
             pltpu.VMEM((context, channels, tokens), real),
             *(coded,) * 5,
-            pltpu.VMEM((replicas, quarter, context, tokens), half),
-            pltpu.VMEM((replicas, context // replicas, channels, tokens), half),
+            by_class,
+            by_class,
             *(coded,) * 4,
-            pltpu.VMEM((replicas, quarter, context, tokens), half),
-            pltpu.VMEM((context, quarter, tokens), real),
-            pltpu.VMEM((replicas, context * quarter, tokens), half),
+            *(by_class,) * 2,
+            pltpu.VMEM((share, channels, tokens), half),
             *(sequences,) * 3,
             *(spectrum,) * 3,
-            *(sequences,) * 3,
-            pltpu.VMEM((quarter, context, tokens), real),
+            *(pltpu.VMEM((context, channels, tokens), real),) * 3,
+            pltpu.VMEM((share, channels, tokens), real),
             pltpu.VMEM((16, width), half),
             pltpu.VMEM((tokens + 8, width), real),
             pltpu.VMEM((tokens, width), real),
@@ -586,13 +611,14 @@
             pltpu.VMEM((8, LANES), real),
             by_position,
             pltpu.VMEM((8, LANES), real),
-            pltpu.VMEM((replicas, context // replicas, LANES), real),
+            pltpu.VMEM((replicas, share, LANES), real),
             *(by_position,) * 4,
-            *(pltpu.VMEM((replicas, 1, LANES), real),) * 2,
+            pltpu.VMEM((replicas, 1, LANES), real),
+            pltpu.VMEM((replicas, share, LANES), real),
             pltpu.SemaphoreType.DMA((ARGUMENTS,)),
             pltpu.SemaphoreType.DMA((6,)),
-            pltpu.SemaphoreType.DMA((22,)),
-            pltpu.SemaphoreType.DMA((22,)),
+            pltpu.SemaphoreType.DMA((23,)),
+            pltpu.SemaphoreType.DMA((23,)),
         ],
         compiler_params=pltpu.CompilerParams(
             collective_id=0, has_side_effects=True, vmem_limit_bytes=63 * 2**20

time: 66.9 us -> 53.3 us (0.80)
  Pallas kernels: 66.1 us -> 52.6 us
    pallas_call x1, Pallas kernels: 63.9 us -> 50.4 us  [per_device(): pl.pallas_call(functools.partial(kernel, context, replicas, grad_scale),...]
where the time goes in v3:
time: 53.3 us; the launch traced here: 53.2 us
  Pallas kernels  52.6 us (99%)
  between operations  0.64 us (1%)
    pallas_call x1, Pallas kernels, per_device(): pl.pallas_call(functools.partial(kernel, context, replicas, grad_scale),...  50.4 us
    pallas_call x1, Pallas kernels, per_device(): pl.pallas_call(settle, out_shape=outputs, in_specs=[pl.BlockSpec(memory_s...  2.18 us

profile of v3, /device:TPU:1, one launch (start us, length us, event | category | flops | bytes accessed | tf_op | source)
XLA Modules:
  0.0 53.2 jit_solution(8250797484665199440)
XLA Ops:
  0.6 50.4 %long_convolution_backward.1 = (bf16[1,128,1024]{2,1,0:T(8,128)(2,1)}, bf16[1,128,1024]{2,1,0:T(8,128)(2,1)}, bf16[1,128,1024]{2,1,0:T(8,128)(2,1)}, f32[128,102...) custom-call(bf16[1,128,1024]{2,1,0:T(8,128)(2,1)} %refs_0_.1, bf16[1,128,1024]{2,1,0:T(8,128)(2,1)} %refs_1_.1, ...), custom_call_target="tpu_custom_call" | custom-call | tf_op jit(solution)/shard_map/long_convolution_backward/pallas_call | solution.py:587
  51.0 2.2 %settle.1 = (bf16[1,128,1024]{2,1,0:T(8,128)(2,1)}, bf16[1,128,1024]{2,1,0:T(8,128)(2,1)}, bf16[1,128,1024]{2,1,0:T(8,128)(2,1)}, f32[128,1024]{1,0:T(8,128)}, f32[3,1024]{1,0:T(4,128)}, /*index=5*/f32[1,1024]{1,0:T(1,128)}) custom-call(bf16[1,128,1024]{2,1,0:T(8,128)(2,1)} %get-tuple-element.18.refs_0_, bf16[1,128,1024]{2,1,0:T(8,128)(2,1)} %get-tuple-element.19.refs_1_, ...), custom_call_target="tpu_custom_call" | custom-call | tf_op jit(solution)/shard_map/settle/pallas_call | solution.py:628

commit v4 on v3

v4 whole, which is shorter than its diff:
```python
import functools
import math

import jax
import jax.numpy as jnp
import ml_dtypes
import numpy as np
from jax import lax
from jax.experimental import pallas as pl
from jax.experimental.pallas import tpu as pltpu
from jax.sharding import PartitionSpec as P

MESH = pl.DeviceIdType.MESH
LANES = 128
PACK = 16
ARGUMENTS = 13
POWER = 32
SHIFT = 125.0
STEPS = 230.0
SMALLEST = 1e-30
HALVES = 2


(
    EDGE,
    FILTER,
    FILTER_STEP,
    FILTER_SHARE,
    FILTER_SHARE_STEP,
    UPSTREAM,
    UPSTREAM_STEP,
    GATED,
    GATED_STEP,
    BACK,
    BACK_STEP,
    CONV,
    CONV_STEP,
    LAG,
    LAG_STEP,
    LAG_HOME,
    LAG_HOME_STEP,
    LAG_SHARE,
    LAG_SHARE_STEP,
    GRAD_EDGE,
    TERMS,
    TERMS_ALL,
    EXCHANGES,
) = range(23)
FILTER_ROW, UPSTREAM_ROW, GATED_ROW, BACK_ROW, CONV_ROW, LAG_ROW, LAG_SUM_ROW = 0, 1, 2, 3, 5, 7, 8


def two_parts(table):
    high = table.astype(ml_dtypes.bfloat16)
    low = (table - high.astype(np.float64)).astype(ml_dtypes.bfloat16)
    return high, low


def tables(blocks, tokens):
    full = blocks * tokens
    shifted = np.arange(blocks) + 0.25
    outer = 2.0 * np.pi * np.outer(shifted, np.arange(blocks)) / blocks
    first = np.concatenate([np.cos(outer), -np.sin(outer)], axis=0)
    last = np.concatenate([np.cos(outer).T, -np.sin(outer).T], axis=1) / full
    twist = 2.0 * np.pi * np.outer(shifted, np.arange(tokens)) / full
    inner = 2.0 * np.pi * np.outer(np.arange(tokens), np.arange(tokens)) / tokens
    cosine, sine = np.cos(inner), np.sin(inner)
    ahead = np.block([[cosine, -sine], [sine, cosine]])
    back = np.block([[cosine, sine], [-sine, cosine]])
    first_high, first_low = two_parts(first)
    last_high, last_low = two_parts(last)
    ahead_high, ahead_low = two_parts(ahead)
    back_high, back_low = two_parts(back)
    return (
        np.concatenate([first_high, first_high, first_low], axis=1),
        np.concatenate([last_high, last_high, last_low], axis=1),
        np.concatenate([ahead_high, ahead_high, ahead_low], axis=0),
        np.concatenate([back_high, back_high, back_low], axis=0),
        np.cos(twist).astype(np.float32),
        np.sin(twist).astype(np.float32),
    )


def encode(value, inverse_step):
    grown = (jnp.abs(value) * inverse_step + 1.0) * 2.0 ** (-SHIFT / POWER)
    for _ in range(POWER.bit_length() - 1):
        grown = grown * grown
    return jnp.where(value < 0.0, -grown, grown).astype(jnp.bfloat16)


def decode(code, step):
    code = code.astype(jnp.float32)
    grown = jnp.exp2((jnp.log2(jnp.abs(code)) + SHIFT) * (1.0 / POWER))
    value = grown * step - step
    return jnp.where(code < 0.0, -value, value)


def step_of(peak):
    top = jnp.max(jnp.max(peak, axis=0, keepdims=True), axis=1, keepdims=True)
    return jnp.broadcast_to(jnp.maximum(top, SMALLEST) * (1.0 / STEPS), (1, LANES))


def peak_of(value):
    rows = jnp.abs(value).reshape(-1, 8, value.shape[-1])
    rows = jnp.max(rows, axis=0)
    peak = rows[:, :LANES]
    for j in range(1, value.shape[-1] // LANES):
        peak = jnp.maximum(peak, rows[:, j * LANES : (j + 1) * LANES])
    return peak


def split_stack(value, axis):
    high = value.astype(jnp.bfloat16)
    low = (value - high.astype(jnp.float32)).astype(jnp.bfloat16)
    return jnp.concatenate([high, low, high], axis=axis)


def forward(source, target, group, first, ahead, twist_cos, twist_sin):
    _, blocks, _ = source.shape
    base, size = group * PACK, PACK * blocks
    rows = jnp.concatenate([source[base + j] for j in range(PACK)], axis=1)
    section = jnp.dot(first[...], split_stack(rows, 0), preferred_element_type=jnp.float32)
    cosine, sine = twist_cos[...], twist_sin[...]
    turned = []
    for j in range(PACK):
        real = section[:blocks, j * LANES : (j + 1) * LANES]
        imag = section[blocks:, j * LANES : (j + 1) * LANES]
        turned.append(jnp.concatenate([real * cosine + imag * sine, imag * cosine - real * sine], axis=1))
    turned = jnp.concatenate(turned, axis=0)
    target[group * size : (group + 1) * size, :] = jnp.dot(
        split_stack(turned, 1), ahead[...], preferred_element_type=jnp.float32
    )


def inverse(left, right, conjugate, target, group, last, back, twist_cos, twist_sin):
    blocks, _, _ = target.shape
    size = PACK * blocks
    rows = slice(group * size, (group + 1) * size)
    a_real, a_imag = left[rows, :LANES], left[rows, LANES:]
    b_real, b_imag = right[rows, :LANES], right[rows, LANES:]
    if conjugate:
        real, imag = a_real * b_real + a_imag * b_imag, a_real * b_imag - a_imag * b_real
    else:
        real, imag = a_real * b_real - a_imag * b_imag, a_real * b_imag + a_imag * b_real
    product = jnp.concatenate([real, imag], axis=1)
    section = jnp.dot(split_stack(product, 1), back[...], preferred_element_type=jnp.float32)
    cosine, sine = twist_cos[...], twist_sin[...]
    turned = []
    for j in range(PACK):
        real = section[j * blocks : (j + 1) * blocks, :LANES]
        imag = section[j * blocks : (j + 1) * blocks, LANES:]
        turned.append(jnp.concatenate([real * cosine - imag * sine, real * sine + imag * cosine], axis=0))
    turned = jnp.concatenate(turned, axis=1)
    result = jnp.dot(last[...], split_stack(turned, 0), preferred_element_type=jnp.float32)
    for j in range(PACK):
        target[:, group * PACK + j, :] = result[:, j * LANES : (j + 1) * LANES]
    return peak_of(result)


def kernel(
    context,
    replicas,
    grad_scale,
    *refs,
):
    given, refs = refs[:ARGUMENTS], refs[ARGUMENTS:]
    outcome, refs = refs[:6], refs[6:]
    held, refs = refs[:ARGUMENTS], refs[ARGUMENTS:]
    (grad_queries, grad_keys_raw, grad_values, grad_long, grad_short, grad_skip), refs = refs[:6], refs[6:]
    queries, keys_raw, values, grad_out, short_filter, long_filter, skip_gain, *constants = held
    first, last, ahead, back, twist_cos, twist_sin = constants
    (
        turned_rows,
        filter_code,
        upstream_code,
        gated_code,
        back_code,
        conv_code,
        lag_code,
        filter_in,
        upstream_in,
        gated_in,
        back_in,
        conv_in,
        lag_in,
        lag_home,
        lag_sum_code,
        filter_seq,
        upstream_seq,
        gated_seq,
        filter_freq,
        upstream_freq,
        gated_freq,
        back_seq,
        conv_seq,
        lag_seq,
        lag_sum,
        key_edge,
        key_ext,
        key_rows,
        grad_key_ext,
        terms,
        terms_in,
        terms_sum,
        terms_all,
        terms_sent,
        steps,
        filter_steps,
        upstream_steps,
        gated_steps,
        back_steps,
        conv_steps,
        lag_steps,
        home_steps,
        load_sem,
        store_sem,
        send_sem,
        recv_sem,
    ) = refs
    tokens, width = key_rows.shape
    channels = filter_seq.shape[0]
    me = lax.axis_index("ctx")
    row = lax.axis_index("dp")
    tiles = width // LANES
    per_tile = LANES // channels
    following = lax.rem(me + 1, context)
    preceding = lax.rem(me + context - 1, context)
    others = pl.ds(0, context - 1)
    peers = pl.ds(0, replicas - 1)

    def over_context(step, start=1, stop=context):
        @pl.loop(start, stop)
        def _(i):
            step(lax.rem(me + i, context))

    def over_replicas(step):
        @pl.loop(1, replicas)
        def _(i):
            step(lax.rem(row + i, replicas))

    def push(source, target, number, half=0, **peer):
        pltpu.make_async_remote_copy(
            src_ref=source,
            dst_ref=target,
            send_sem=send_sem.at[half, number],
            recv_sem=recv_sem.at[half, number],
            device_id=peer,
            device_id_type=MESH,
        ).start()

    def keep(source, target, number, half=0):
        pltpu.make_async_copy(source, target, recv_sem.at[half, number]).start()

    def arrived(extent, number, half=0):
        pltpu.make_async_copy(extent, extent, recv_sem.at[half, number]).wait()

    def sent(extent, number, half=0):
        pltpu.make_async_copy(extent, extent, send_sem.at[half, number]).wait()

    def lane_tiles(step):
        for t in range(tiles):
            step(t, slice(t * LANES, (t + 1) * LANES))

    def upstream_of(lanes):
        return grad_out[0, :, lanes].astype(jnp.float32) * queries[0, :, lanes].astype(jnp.float32)

    def hold_step(number, peak):
        step = step_of(peak)
        steps[number : number + 1, :] = step
        return 1.0 / step

    def code_rows(make, code, number):
        peak = jnp.zeros((8, LANES), jnp.float32)
        for t in range(tiles):
            part = make(slice(t * LANES, (t + 1) * LANES)).T
            turned_rows[t * per_tile : (t + 1) * per_tile] = part.reshape(per_tile, channels, tokens)
            peak = jnp.maximum(peak, peak_of(part))
        inverse_step = hold_step(number, peak)
        for p in range(context):
            block = encode(turned_rows[p], inverse_step)
            if len(code.shape) == 3:
                code[p] = block
            else:
                for half in range(HALVES):
                    code[half, p] = block[half * PACK : (half + 1) * PACK]

    def open_half(code_in, found_steps, sequences, half):
        for p in range(context):
            sequences[half * PACK : (half + 1) * PACK, p] = decode(code_in[half, p], found_steps[p])

    def exchange(code, code_in, number, half, step_row=None, steps_in=None):
        count = 0 if steps_in is None else steps_in.shape[1]

        def one(p):
            push(code.at[half, p], code_in.at[half, me], number, half, ctx=p)
            if count:
                push(steps.at[pl.ds(step_row, count)], steps_in.at[me], number + 1, ctx=p)

        over_context(one)
        keep(code.at[half, me], code_in.at[half, me], number, half)
        if count:
            keep(steps.at[pl.ds(step_row, count)], steps_in.at[me], number + 1)

    def result_half(left, right, conjugate, sequences, code, row_number, half):
        peak = inverse(left, right, conjugate, sequences, half, last, back, twist_cos, twist_sin)
        inverse_step = hold_step(row_number + half, peak)
        for p in range(context):
            code[half, p] = encode(sequences[p, half * PACK : (half + 1) * PACK], inverse_step)

    def store(i):
        made = (grad_queries, grad_keys_raw, grad_values, grad_long, grad_short, grad_skip)[i]
        return pltpu.make_async_copy(made, outcome[i], store_sem.at[i])

    def load(i):
        return pltpu.make_async_copy(given[i], held[i], load_sem.at[i])

    order = (5, 3, 0, 1, 2, 4, 6, 7, 9, 11, 12, 8, 10)
    for i in order:
        load(i).start()
    barrier = pltpu.get_barrier_semaphore()
    over_context(lambda p: pl.semaphore_signal(barrier, inc=1, device_id={"ctx": p}, device_id_type=MESH))
    over_replicas(lambda p: pl.semaphore_signal(barrier, inc=1, device_id={"dp": p}, device_id_type=MESH))

    load(5).wait()
    code_rows(lambda lanes: long_filter[:, lanes], filter_code, FILTER_ROW)
    load(3).wait()
    load(0).wait()
    code_rows(upstream_of, upstream_code, UPSTREAM_ROW)
    pl.semaphore_wait(barrier, context - 1 + replicas - 1)

    push(given[1].at[0, pl.ds(tokens - 16, 16)], key_edge, EDGE, ctx=following)

    share = context // replicas
    part_size = share // 2
    sender_class = lax.rem(me, replicas)
    side = lax.rem(me // replicas, 2)
    place = side * part_size + me // (2 * replicas)
    taken = lax.rem(row + context - sender_class, replicas)
    own_block = taken == sender_class
    sides = (side, 1 - side)

    def over_class(source_of, target, step_row, steps_in, number):
        for far in (1, 0):

            @pl.loop(0, part_size)
            def _(j):
                i = 2 * j + sides[far]
                p = taken + i * replicas

                @pl.when(p != me)
                def _():
                    push(source_of(i, p), target.at[sender_class, place], number, far, ctx=p)
                    push(
                        steps.at[pl.ds(step_row, 1)], steps_in.at[sender_class, pl.ds(place, 1)], number + 1, far, ctx=p
                    )

                if far == 0:

                    @pl.when(p == me)
                    def _():
                        keep(source_of(i, p), target.at[sender_class, place], number)
                        keep(steps.at[pl.ds(step_row, 1)], steps_in.at[sender_class, pl.ds(place, 1)], number + 1)

    def share_class(blocks, found_steps, number, share_number):
        for far in (0, 1):
            rows = pl.ds(sides[far] * part_size, part_size)
            arrived(blocks.at[taken, rows], number, far)
            arrived(found_steps.at[taken, rows], number + 1, far)

            def one(p):
                push(blocks.at[taken, rows], blocks.at[taken, rows], share_number, far, dp=p)
                push(found_steps.at[taken, rows], found_steps.at[taken, rows], share_number + 1, far, dp=p)

            over_replicas(one)

    def shared(blocks, found_steps, share_number):
        for far in (0, 1):
            arrived(blocks.at[peers, pl.ds(0, part_size)], share_number, far)
            arrived(found_steps.at[peers, pl.ds(0, part_size)], share_number + 1, far)

    def class_of(p):
        return p % replicas, (p // replicas) % 2 * part_size + p // (2 * replicas)

    over_class(lambda i, p: filter_code.at[p], filter_in, FILTER_ROW, filter_steps, FILTER)
    exchange(upstream_code, upstream_in, UPSTREAM, 0, UPSTREAM_ROW, upstream_steps)
    exchange(upstream_code, upstream_in, UPSTREAM, 1)

    load(1).wait()
    load(2).wait()
    load(4).wait()
    key_ext[pl.ds(8, tokens), :] = keys_raw[0].astype(jnp.float32)
    arrived(key_edge, EDGE)
    edge = key_edge[...].astype(jnp.float32)[8:]
    key_ext[pl.ds(0, 8), :] = jnp.where(me == 0, 0.0, edge)

    def gated_of(lanes):
        rows = (
            short_filter[0:1, lanes] * key_ext[pl.ds(8, tokens), lanes]
            + short_filter[1:2, lanes] * key_ext[pl.ds(7, tokens), lanes]
            + short_filter[2:3, lanes] * key_ext[pl.ds(6, tokens), lanes]
        )
        key_rows[:, lanes] = rows
        return rows * values[0, :, lanes].astype(jnp.float32)

    code_rows(gated_of, gated_code, GATED_ROW)
    exchange(gated_code, gated_in, GATED, 0, GATED_ROW, gated_steps)
    exchange(gated_code, gated_in, GATED, 1)

    share_class(filter_in, filter_steps, FILTER, FILTER_SHARE)

    for i in range(6, ARGUMENTS):
        load(i).wait()

    def ahead_half(code_in, found_steps, sequences, spectrum, half):
        open_half(code_in, found_steps, sequences, half)
        forward(sequences, spectrum, half, first, ahead, twist_cos, twist_sin)

    arrived(upstream_in.at[0], UPSTREAM, 0)
    arrived(upstream_steps, UPSTREAM_STEP, 0)
    ahead_half(upstream_in, upstream_steps, upstream_seq, upstream_freq, 0)
    shared(filter_in, filter_steps, FILTER_SHARE)
    for p in range(context):
        sender, part = class_of(p)
        filter_seq[:, p] = decode(filter_in[sender, part], filter_steps[sender, part : part + 1, :])

    for half in range(HALVES):
        if half > 0:
            arrived(upstream_in.at[half], UPSTREAM, half)
            ahead_half(upstream_in, upstream_steps, upstream_seq, upstream_freq, half)
        forward(filter_seq, filter_freq, half, first, ahead, twist_cos, twist_sin)
        result_half(filter_freq, upstream_freq, True, back_seq, back_code, BACK_ROW, half)
        if half == 0:
            exchange(back_code, back_in, BACK, half)
        else:
            exchange(back_code, back_in, BACK, half, BACK_ROW, back_steps)

    for half in range(HALVES):
        arrived(gated_in.at[half], GATED, half)
        if half == 0:
            arrived(gated_steps, GATED_STEP)
        ahead_half(gated_in, gated_steps, gated_seq, gated_freq, half)

    peak = jnp.zeros((8, LANES), jnp.float32)
    for half in range(HALVES):
        found = inverse(gated_freq, upstream_freq, True, lag_seq, half, last, back, twist_cos, twist_sin)
        peak = jnp.maximum(peak, found)
    inverse_step = hold_step(LAG_ROW, peak)
    for part in range(context // replicas):
        for c in range(replicas):
            lag_code[c, part] = encode(lag_seq[part * replicas + c], inverse_step)

    def share_lag(p):
        push(lag_code.at[lax.rem(p + context - sender_class, replicas)], lag_in.at[row], LAG, dp=p)
        push(steps.at[pl.ds(LAG_ROW, 1)], lag_steps.at[row], LAG_STEP, dp=p)

    over_replicas(share_lag)
    keep(lag_code.at[taken], lag_in.at[row], LAG)
    keep(steps.at[pl.ds(LAG_ROW, 1)], lag_steps.at[row], LAG_STEP)

    for half in range(HALVES):
        result_half(filter_freq, gated_freq, False, conv_seq, conv_code, CONV_ROW, half)
        if half == 0:
            exchange(conv_code, conv_in, CONV, half)

    def home_rows(code_in, found_steps, t):
        parts = [
            decode(code_in[half, p], found_steps[p, half : half + 1, :])
            for p in range(t * per_tile, (t + 1) * per_tile)
            for half in range(HALVES)
        ]
        return jnp.concatenate(parts, axis=0).T

    for half in range(HALVES):
        arrived(back_in.at[half], BACK, half)
    arrived(back_steps, BACK_STEP)

    def use_back(t, lanes):
        back_rows = home_rows(back_in, back_steps, t)
        upstream = upstream_of(lanes)
        grad_gated = back_rows + skip_gain[:, lanes] * upstream
        rows = key_rows[:, lanes]
        value_rows = values[0, :, lanes].astype(jnp.float32)
        grad_values[0, :, lanes] = (grad_gated * rows).astype(jnp.bfloat16)
        grad_rows = grad_gated * value_rows
        grad_key_ext[pl.ds(0, tokens), lanes] = grad_rows
        for j in range(3):
            terms[t, j : j + 1, :] = jnp.sum(
                grad_rows * key_ext[pl.ds(8 - j, tokens), lanes], axis=0, keepdims=True
            )
        terms[t, 3:4, :] = jnp.sum(upstream * (rows * value_rows), axis=0, keepdims=True)

    lane_tiles(use_back)
    spacing = 2 * context // tiles
    owned = me // spacing * 2 + lax.rem(me, spacing) // (spacing // 2)
    owner = me == owned // 2 * spacing + spacing // 4 + lax.rem(owned, 2) * (spacing // 4)

    @pl.loop(0, tiles)
    def _(i):
        t = lax.rem(me + i, tiles)
        p = t // 2 * spacing + spacing // 4 + lax.rem(t, 2) * (spacing // 4)

        @pl.when(p != me)
        def _():
            push(terms.at[t], terms_in.at[me], TERMS, ctx=p)

        @pl.when(p == me)
        def _():
            keep(terms.at[t], terms_in.at[me], TERMS)

    push(grad_key_ext.at[pl.ds(0, 8)], grad_key_ext.at[pl.ds(tokens, 8)], GRAD_EDGE, ctx=preceding)
    exchange(conv_code, conv_in, CONV, 1, CONV_ROW, conv_steps)
    store(2).start()

    arrived(lag_in, LAG)
    arrived(lag_steps, LAG_STEP)
    peak = jnp.zeros((8, LANES), jnp.float32)
    for part in range(context // replicas):
        total = decode(lag_in[0, part], lag_steps[0])
        for j in range(1, replicas):
            total = total + decode(lag_in[j, part], lag_steps[j])
        lag_sum[part] = total
        peak = jnp.maximum(peak, peak_of(total))
    inverse_step = hold_step(LAG_SUM_ROW, peak)
    for part in range(context // replicas):
        lag_sum_code[part] = encode(lag_sum[part], inverse_step)

    over_class(lambda i, p: lag_sum_code.at[i], lag_home, LAG_SUM_ROW, home_steps, LAG_HOME)

    @pl.when(owner)
    def _():
        arrived(terms_in, TERMS)
        total = terms_in[0]
        for p in range(1, context):
            total = total + terms_in[p]
        terms_sum[...] = total

        for j in (2, 1, 3):
            there = lax.rem(row + j, replicas)

            @pl.loop(0, context)
            def _(p):
                push(terms_sum, terms_all.at[row, owned], TERMS_ALL, dp=there, ctx=lax.rem(me + p, context))

        over_context(lambda p: push(terms_sum, terms_all.at[row, owned], TERMS_ALL, ctx=p))
        keep(terms_sum, terms_all.at[row, owned], TERMS_ALL)

    arrived(grad_key_ext.at[pl.ds(tokens, 8)], GRAD_EDGE)
    grad_key_ext[pl.ds(tokens, 8), :] = jnp.where(me == context - 1, 0.0, grad_key_ext[pl.ds(tokens, 8), :])

    def make_keys(t, lanes):
        grad_keys_raw[0, :, lanes] = (
            short_filter[0:1, lanes] * grad_key_ext[pl.ds(0, tokens), lanes]
            + short_filter[1:2, lanes] * grad_key_ext[pl.ds(1, tokens), lanes]
            + short_filter[2:3, lanes] * grad_key_ext[pl.ds(2, tokens), lanes]
        ).astype(jnp.bfloat16)

    lane_tiles(make_keys)
    store(1).start()

    share_class(lag_home, home_steps, LAG_HOME, LAG_SHARE)

    for half in range(HALVES):
        arrived(conv_in.at[half], CONV, half)
    arrived(conv_steps, CONV_STEP)

    def use_conv(t, lanes):
        conv_rows = home_rows(conv_in, conv_steps, t)
        gated = key_rows[:, lanes] * values[0, :, lanes].astype(jnp.float32)
        grad_queries[0, :, lanes] = (
            grad_out[0, :, lanes].astype(jnp.float32) * (conv_rows + skip_gain[:, lanes] * gated)
        ).astype(jnp.bfloat16)

    lane_tiles(use_conv)
    store(0).start()


    shared(lag_home, home_steps, LAG_SHARE)

    def use_lag(t, lanes):
        parts = []
        for p in range(t * per_tile, (t + 1) * per_tile):
            sender, part = class_of(p)
            parts.append(decode(lag_home[sender, part], home_steps[sender, part : part + 1, :]))
        grad_long[:, lanes] = jnp.concatenate(parts, axis=0).T * grad_scale

    lane_tiles(use_lag)
    store(3).start()

    arrived(terms_all, TERMS_ALL)
    for t in range(tiles):
        lanes = slice(t * LANES, (t + 1) * LANES)
        total = terms_all[0, t]
        for j in range(1, replicas):
            total = total + terms_all[j, t]
        total = total * grad_scale
        grad_short[:, lanes] = total[:3]
        grad_skip[:, lanes] = total[3:4]
    store(4).start()
    store(5).start()
    for i in range(6):
        store(i).wait()

    sent(key_edge, EDGE)

    @pl.when(own_block)
    def _():
        for number in (FILTER, LAG_HOME):
            sent(filter_in.at[0, pl.ds(0, part_size - 1)], number)
            sent(filter_steps.at[0, pl.ds(0, part_size - 1)], number + 1)

    @pl.when(jnp.logical_not(own_block))
    def _():
        for number in (FILTER, LAG_HOME):
            sent(filter_in.at[0, pl.ds(0, part_size)], number)
            sent(filter_steps.at[0, pl.ds(0, part_size)], number + 1)

    for number in (FILTER, LAG_HOME):
        sent(filter_in.at[0, pl.ds(0, part_size)], number, 1)
        sent(filter_steps.at[0, pl.ds(0, part_size)], number + 1, 1)
    for number in (FILTER_SHARE, LAG_SHARE):
        for far in (0, 1):
            sent(filter_in.at[peers, pl.ds(0, part_size)], number, far)
            sent(filter_steps.at[peers, pl.ds(0, part_size)], number + 1, far)
    for half in range(HALVES):
        for number in (UPSTREAM, GATED, BACK, CONV):
            sent(upstream_in.at[0, others], number, half)
    for number in (UPSTREAM, GATED):
        sent(upstream_steps.at[others], number + 1)
    for number in (BACK, CONV):
        sent(back_steps.at[others], number + 1)
    sent(lag_in.at[peers], LAG)
    sent(lag_steps.at[peers], LAG_STEP)
    sent(grad_key_ext.at[pl.ds(tokens, 8)], GRAD_EDGE)

    @pl.when(owner)
    def _():
        sent(terms.at[pl.ds(0, tiles - 1)], TERMS)
        sent(terms_sent.at[pl.ds(0, replicas * context - 1)], TERMS_ALL)

    @pl.when(jnp.logical_not(owner))
    def _():
        sent(terms, TERMS)


def settle(*refs):
    count = (len(refs) - 2) // 3
    given, made, held = refs[:count], refs[count : 2 * count], refs[2 * count : 3 * count]
    loads = [pltpu.make_async_copy(given[i], held[i], refs[-2].at[i]) for i in range(count)]
    stores = [pltpu.make_async_copy(held[i], made[i], refs[-1].at[i]) for i in range(count)]
    for copy in loads:
        copy.start()
    for load, store in zip(loads, stores):
        load.wait()
        store.start()
    for copy in stores:
        copy.wait()


def per_device(context, replicas, queries, keys_raw, values, grad_out, short_filter, long_filter, skip_gain):
    _, tokens, width = queries.shape
    channels = width // context
    share = context // replicas
    constants = [jnp.asarray(table) for table in tables(context, tokens)]
    grad_scale = 1.0 / math.sqrt(replicas * context * tokens)
    real = jnp.float32
    half = jnp.bfloat16
    by_class = pltpu.VMEM((replicas, share, channels, tokens), half)
    coded = pltpu.VMEM((HALVES, context, channels // HALVES, tokens), half)
    sequences = pltpu.VMEM((channels, context, tokens), real)
    spectrum = pltpu.VMEM((channels * context, 2 * tokens), real)
    outputs = (
        jax.ShapeDtypeStruct(queries.shape, jnp.bfloat16),
        jax.ShapeDtypeStruct(queries.shape, jnp.bfloat16),
        jax.ShapeDtypeStruct(queries.shape, jnp.bfloat16),
        jax.ShapeDtypeStruct((tokens, width), real),
        jax.ShapeDtypeStruct((3, width), real),
        jax.ShapeDtypeStruct((1, width), real),
    )
    arguments = (queries, keys_raw, values, grad_out, short_filter, long_filter, skip_gain.reshape(1, width), *constants)
    results = pl.pallas_call(
        functools.partial(kernel, context, replicas, grad_scale),
        out_shape=outputs,
        in_specs=[pl.BlockSpec(memory_space=pltpu.HBM)] * ARGUMENTS,
        out_specs=(pl.BlockSpec(memory_space=pltpu.HBM),) * 6,
        scratch_shapes=[
            *(pltpu.VMEM(argument.shape, argument.dtype) for argument in arguments),
            *(pltpu.VMEM(output.shape, output.dtype) for output in outputs),
            pltpu.VMEM((context, channels, tokens), real),
            pltpu.VMEM((context, channels, tokens), half),
            *(coded,) * 4,
            by_class,
            by_class,
            *(coded,) * 4,
            *(by_class,) * 2,
            pltpu.VMEM((share, channels, tokens), half),
            *(sequences,) * 3,
            *(spectrum,) * 3,
            *(pltpu.VMEM((context, channels, tokens), real),) * 3,
            pltpu.VMEM((share, channels, tokens), real),
            pltpu.VMEM((16, width), half),
            pltpu.VMEM((tokens + 8, width), real),
            pltpu.VMEM((tokens, width), real),
            pltpu.VMEM((tokens + 8, width), real),
            pltpu.VMEM((width // LANES, 4, LANES), real),
            pltpu.VMEM((context, 4, LANES), real),
            pltpu.VMEM((4, LANES), real),
            pltpu.VMEM((replicas, width // LANES, 4, LANES), real),
            pltpu.VMEM((replicas * context, 4, LANES), real),
            pltpu.VMEM((16, LANES), real),
            pltpu.VMEM((replicas, share, LANES), real),
            *(pltpu.VMEM((context, 1, LANES), real),) * 2,
            *(pltpu.VMEM((context, HALVES, LANES), real),) * 2,
            pltpu.VMEM((replicas, 1, LANES), real),
            pltpu.VMEM((replicas, share, LANES), real),
            pltpu.SemaphoreType.DMA((ARGUMENTS,)),
            pltpu.SemaphoreType.DMA((6,)),
            pltpu.SemaphoreType.DMA((HALVES, EXCHANGES)),
            pltpu.SemaphoreType.DMA((HALVES, EXCHANGES)),
        ],
        compiler_params=pltpu.CompilerParams(
            collective_id=0, has_side_effects=True, vmem_limit_bytes=63 * 2**20
        ),
        name="long_convolution_backward",
    )(*arguments)
    results = pl.pallas_call(
        settle,
        out_shape=outputs,
        in_specs=[pl.BlockSpec(memory_space=pltpu.HBM)] * len(results),
        out_specs=(pl.BlockSpec(memory_space=pltpu.HBM),) * len(results),
        scratch_shapes=[
            *(pltpu.VMEM(result.shape, result.dtype) for result in results),
            pltpu.SemaphoreType.DMA((len(results),)),
            pltpu.SemaphoreType.DMA((len(results),)),
        ],
        compiler_params=pltpu.CompilerParams(vmem_limit_bytes=63 * 2**20),
        name="settle",
    )(*results)
    grad_queries, grad_keys_raw, grad_values, grad_long, grad_short, grad_skip = results
    return grad_queries, grad_keys_raw, grad_values, grad_long, grad_short, grad_skip.reshape(width)


def solution(mesh):
    rows = P("dp", "ctx", "chan")
    return jax.shard_map(
        functools.partial(per_device, mesh.shape["ctx"], mesh.shape["dp"]),
        mesh=mesh,
        in_specs=(rows, rows, rows, rows, P(None, "chan"), P("ctx", "chan"), P("chan")),
        out_specs=(rows, rows, rows, P("ctx", "chan"), P(None, "chan"), P("chan")),
        check_vma=False,
    )
```

time: 53.3 us -> 51 us (0.957)
  Pallas kernels: 52.6 us -> 50.3 us
    pallas_call x1, Pallas kernels: 50.4 us -> 48.1 us  [per_device(): pl.pallas_call(functools.partial(kernel, context, replicas, grad_scale),...]
where the time goes in v4:
time: 51 us; the launch traced here: 50.9 us
  Pallas kernels  50.3 us (99%)
  between operations  0.64 us (1%)
    pallas_call x1, Pallas kernels, per_device(): pl.pallas_call(functools.partial(kernel, context, replicas, grad_scale),...  48.1 us
    pallas_call x1, Pallas kernels, per_device(): pl.pallas_call(settle, out_shape=outputs, in_specs=[pl.BlockSpec(memory_s...  2.18 us

profile of v4, /device:TPU:1, one launch (start us, length us, event | category | flops | bytes accessed | tf_op | source)
XLA Modules:
  0.0 50.9 jit_solution(17237268656000857368)
XLA Ops:
  0.6 48.1 %long_convolution_backward.1 = (bf16[1,128,1024]{2,1,0:T(8,128)(2,1)}, bf16[1,128,1024]{2,1,0:T(8,128)(2,1)}, bf16[1,128,1024]{2,1,0:T(8,128)(2,1)}, f32[128,102...) custom-call(bf16[1,128,1024]{2,1,0:T(8,128)(2,1)} %refs_0_.1, bf16[1,128,1024]{2,1,0:T(8,128)(2,1)} %refs_1_.1, ...), custom_call_target="tpu_custom_call" | custom-call | tf_op jit(solution)/shard_map/long_convolution_backward/pallas_call | solution.py:679
  48.7 2.2 %settle.1 = (bf16[1,128,1024]{2,1,0:T(8,128)(2,1)}, bf16[1,128,1024]{2,1,0:T(8,128)(2,1)}, bf16[1,128,1024]{2,1,0:T(8,128)(2,1)}, f32[128,1024]{1,0:T(8,128)}, f32[3,1024]{1,0:T(4,128)}, /*index=5*/f32[1,1024]{1,0:T(1,128)}) custom-call(bf16[1,128,1024]{2,1,0:T(8,128)(2,1)} %get-tuple-element.18.refs_0_, bf16[1,128,1024]{2,1,0:T(8,128)(2,1)} %get-tuple-element.19.refs_1_, ...), custom_call_target="tpu_custom_call" | custom-call | tf_op jit(solution)/shard_map/settle/pallas_call | solution.py:724

commit v5 on v4

--- a/solution.py
+++ b/solution.py
@@ -402,10 +402,9 @@
         return rows * values[0, :, lanes].astype(jnp.float32)
 
     code_rows(gated_of, gated_code, GATED_ROW)
+    share_class(filter_in, filter_steps, FILTER, FILTER_SHARE)
     exchange(gated_code, gated_in, GATED, 0, GATED_ROW, gated_steps)
     exchange(gated_code, gated_in, GATED, 1)
-
-    share_class(filter_in, filter_steps, FILTER, FILTER_SHARE)
 
     for i in range(6, ARGUMENTS):
         load(i).wait()
@@ -433,17 +432,16 @@
         else:
             exchange(back_code, back_in, BACK, half, BACK_ROW, back_steps)
 
+    lag_peak = jnp.zeros((8, LANES), jnp.float32)
     for half in range(HALVES):
         arrived(gated_in.at[half], GATED, half)
         if half == 0:
             arrived(gated_steps, GATED_STEP)
         ahead_half(gated_in, gated_steps, gated_seq, gated_freq, half)
-
-    peak = jnp.zeros((8, LANES), jnp.float32)
-    for half in range(HALVES):
         found = inverse(gated_freq, upstream_freq, True, lag_seq, half, last, back, twist_cos, twist_sin)
-        peak = jnp.maximum(peak, found)
-    inverse_step = hold_step(LAG_ROW, peak)
+        lag_peak = jnp.maximum(lag_peak, found)
+
+    inverse_step = hold_step(LAG_ROW, lag_peak)
     for part in range(context // replicas):
         for c in range(replicas):
             lag_code[c, part] = encode(lag_seq[part * replicas + c], inverse_step)
@@ -507,7 +505,6 @@
             keep(terms.at[t], terms_in.at[me], TERMS)
 
     push(grad_key_ext.at[pl.ds(0, 8)], grad_key_ext.at[pl.ds(tokens, 8)], GRAD_EDGE, ctx=preceding)
-    exchange(conv_code, conv_in, CONV, 1, CONV_ROW, conv_steps)
     store(2).start()
 
     arrived(lag_in, LAG)
@@ -524,6 +521,8 @@
         lag_sum_code[part] = encode(lag_sum[part], inverse_step)
 
     over_class(lambda i, p: lag_sum_code.at[i], lag_home, LAG_SUM_ROW, home_steps, LAG_HOME)
+
+    exchange(conv_code, conv_in, CONV, 1, CONV_ROW, conv_steps)
 
     @pl.when(owner)
     def _():

time: 51 us -> 49.4 us (0.969)
  Pallas kernels: 50.3 us -> 48.6 us
    pallas_call x1, Pallas kernels: 48.1 us -> 46.4 us  [per_device(): pl.pallas_call(functools.partial(kernel, context, replicas, grad_scale),...]
where the time goes in v5:
time: 49.4 us; the launch traced here: 49.3 us
  Pallas kernels  48.6 us (98%)
  between operations  0.64 us (1%)
    pallas_call x1, Pallas kernels, per_device(): pl.pallas_call(functools.partial(kernel, context, replicas, grad_scale),...  46.4 us
    pallas_call x1, Pallas kernels, per_device(): pl.pallas_call(settle, out_shape=outputs, in_specs=[pl.BlockSpec(memory_s...  2.18 us

profile of v5, /device:TPU:1, one launch (start us, length us, event | category | flops | bytes accessed | tf_op | source)
XLA Modules:
  0.0 49.3 jit_solution(15379153904414641716)
XLA Ops:
  0.6 46.4 %long_convolution_backward.1 = (bf16[1,128,1024]{2,1,0:T(8,128)(2,1)}, bf16[1,128,1024]{2,1,0:T(8,128)(2,1)}, bf16[1,128,1024]{2,1,0:T(8,128)(2,1)}, f32[128,102...) custom-call(bf16[1,128,1024]{2,1,0:T(8,128)(2,1)} %refs_0_.1, bf16[1,128,1024]{2,1,0:T(8,128)(2,1)} %refs_1_.1, ...), custom_call_target="tpu_custom_call" | custom-call | tf_op jit(solution)/shard_map/long_convolution_backward/pallas_call | solution.py:678
  47.1 2.2 %settle.1 = (bf16[1,128,1024]{2,1,0:T(8,128)(2,1)}, bf16[1,128,1024]{2,1,0:T(8,128)(2,1)}, bf16[1,128,1024]{2,1,0:T(8,128)(2,1)}, f32[128,1024]{1,0:T(8,128)}, f32[3,1024]{1,0:T(4,128)}, /*index=5*/f32[1,1024]{1,0:T(1,128)}) custom-call(bf16[1,128,1024]{2,1,0:T(8,128)(2,1)} %get-tuple-element.18.refs_0_, bf16[1,128,1024]{2,1,0:T(8,128)(2,1)} %get-tuple-element.19.refs_1_, ...), custom_call_target="tpu_custom_call" | custom-call | tf_op jit(solution)/shard_map/settle/pallas_call | solution.py:723

commit v6 on v5

--- a/solution.py
+++ b/solution.py
@@ -17,7 +17,7 @@
 POWER = 32
 SHIFT = 125.0
 STEPS = 230.0
-SMALLEST = 1e-30
+SMALLEST = 1e-35
 HALVES = 2
 
 
@@ -227,8 +227,8 @@
     others = pl.ds(0, context - 1)
     peers = pl.ds(0, replicas - 1)
 
-    def over_context(step, start=1, stop=context):
-        @pl.loop(start, stop)
+    def over_context(step):
+        @pl.loop(1, context)
         def _(i):
             step(lax.rem(me + i, context))
 
@@ -583,20 +583,6 @@
 
     lane_tiles(use_lag)
     store(3).start()
-
-    arrived(terms_all, TERMS_ALL)
-    for t in range(tiles):
-        lanes = slice(t * LANES, (t + 1) * LANES)
-        total = terms_all[0, t]
-        for j in range(1, replicas):
-            total = total + terms_all[j, t]
-        total = total * grad_scale
-        grad_short[:, lanes] = total[:3]
-        grad_skip[:, lanes] = total[3:4]
-    store(4).start()
-    store(5).start()
-    for i in range(6):
-        store(i).wait()
 
     sent(key_edge, EDGE)
 
@@ -638,6 +624,22 @@
     @pl.when(jnp.logical_not(owner))
     def _():
         sent(terms, TERMS)
+
+    for i in range(4):
+        store(i).wait()
+    arrived(terms_all, TERMS_ALL)
+    for t in range(tiles):
+        lanes = slice(t * LANES, (t + 1) * LANES)
+        total = terms_all[0, t]
+        for j in range(1, replicas):
+            total = total + terms_all[j, t]
+        total = total * grad_scale
+        grad_short[:, lanes] = total[:3]
+        grad_skip[:, lanes] = total[3:4]
+    store(4).start()
+    store(5).start()
+    store(4).wait()
+    store(5).wait()
 
 
 def settle(*refs):

time: 49.4 us -> 49.4 us (level)
  no operation moved by 1% of the time
where the time goes in v6:
time: 49.4 us; the launch traced here: 49.2 us
  Pallas kernels  48.6 us (98%)
  between operations  0.64 us (1%)
    pallas_call x1, Pallas kernels, per_device(): pl.pallas_call(functools.partial(kernel, context, replicas, grad_scale),...  46.4 us
    pallas_call x1, Pallas kernels, per_device(): pl.pallas_call(settle, out_shape=outputs, in_specs=[pl.BlockSpec(memory_s...  2.18 us

profile of v6, /device:TPU:1, one launch (start us, length us, event | category | flops | bytes accessed | tf_op | source)
XLA Modules:
  0.0 49.2 jit_solution(9040504921575712765)
XLA Ops:
  0.6 46.4 %long_convolution_backward.1 = (bf16[1,128,1024]{2,1,0:T(8,128)(2,1)}, bf16[1,128,1024]{2,1,0:T(8,128)(2,1)}, bf16[1,128,1024]{2,1,0:T(8,128)(2,1)}, f32[128,102...) custom-call(bf16[1,128,1024]{2,1,0:T(8,128)(2,1)} %refs_0_.1, bf16[1,128,1024]{2,1,0:T(8,128)(2,1)} %refs_1_.1, ...), custom_call_target="tpu_custom_call" | custom-call | tf_op jit(solution)/shard_map/long_convolution_backward/pallas_call | solution.py:680
  47.0 2.2 %settle.1 = (bf16[1,128,1024]{2,1,0:T(8,128)(2,1)}, bf16[1,128,1024]{2,1,0:T(8,128)(2,1)}, bf16[1,128,1024]{2,1,0:T(8,128)(2,1)}, f32[128,1024]{1,0:T(8,128)}, f32[3,1024]{1,0:T(4,128)}, /*index=5*/f32[1,1024]{1,0:T(1,128)}) custom-call(bf16[1,128,1024]{2,1,0:T(8,128)(2,1)} %get-tuple-element.18.refs_0_, bf16[1,128,1024]{2,1,0:T(8,128)(2,1)} %get-tuple-element.19.refs_1_, ...), custom_call_target="tpu_custom_call" | custom-call | tf_op jit(solution)/shard_map/settle/pallas_call | solution.py:725

commit v7 on v6

--- a/solution.py
+++ b/solution.py
@@ -327,7 +327,9 @@
     code_rows(upstream_of, upstream_code, UPSTREAM_ROW)
     pl.semaphore_wait(barrier, context - 1 + replicas - 1)
 
-    push(given[1].at[0, pl.ds(tokens - 16, 16)], key_edge, EDGE, ctx=following)
+    @pl.when(me < context - 1)
+    def _():
+        push(given[1].at[0, pl.ds(tokens - 16, 16)], key_edge, EDGE, ctx=following)
 
     share = context // replicas
     part_size = share // 2
@@ -388,9 +390,15 @@
     load(2).wait()
     load(4).wait()
     key_ext[pl.ds(8, tokens), :] = keys_raw[0].astype(jnp.float32)
-    arrived(key_edge, EDGE)
-    edge = key_edge[...].astype(jnp.float32)[8:]
-    key_ext[pl.ds(0, 8), :] = jnp.where(me == 0, 0.0, edge)
+
+    @pl.when(me == 0)
+    def _():
+        key_ext[pl.ds(0, 8), :] = jnp.zeros((8, width), jnp.float32)
+
+    @pl.when(me > 0)
+    def _():
+        arrived(key_edge, EDGE)
+        key_ext[pl.ds(0, 8), :] = key_edge[...].astype(jnp.float32)[8:]
 
     def gated_of(lanes):
         rows = (
@@ -504,7 +512,10 @@
         def _():
             keep(terms.at[t], terms_in.at[me], TERMS)
 
-    push(grad_key_ext.at[pl.ds(0, 8)], grad_key_ext.at[pl.ds(tokens, 8)], GRAD_EDGE, ctx=preceding)
+    @pl.when(me > 0)
+    def _():
+        push(grad_key_ext.at[pl.ds(0, 8)], grad_key_ext.at[pl.ds(tokens, 8)], GRAD_EDGE, ctx=preceding)
+
     store(2).start()
 
     arrived(lag_in, LAG)
@@ -542,8 +553,13 @@
         over_context(lambda p: push(terms_sum, terms_all.at[row, owned], TERMS_ALL, ctx=p))
         keep(terms_sum, terms_all.at[row, owned], TERMS_ALL)
 
-    arrived(grad_key_ext.at[pl.ds(tokens, 8)], GRAD_EDGE)
-    grad_key_ext[pl.ds(tokens, 8), :] = jnp.where(me == context - 1, 0.0, grad_key_ext[pl.ds(tokens, 8), :])
+    @pl.when(me < context - 1)
+    def _():
+        arrived(grad_key_ext.at[pl.ds(tokens, 8)], GRAD_EDGE)
+
+    @pl.when(me == context - 1)
+    def _():
+        grad_key_ext[pl.ds(tokens, 8), :] = jnp.zeros((8, width), jnp.float32)
 
     def make_keys(t, lanes):
         grad_keys_raw[0, :, lanes] = (
@@ -584,7 +600,9 @@
     lane_tiles(use_lag)
     store(3).start()
 
-    sent(key_edge, EDGE)
+    @pl.when(me < context - 1)
+    def _():
+        sent(key_edge, EDGE)
 
     @pl.when(own_block)
     def _():
@@ -614,7 +632,11 @@
         sent(back_steps.at[others], number + 1)
     sent(lag_in.at[peers], LAG)
     sent(lag_steps.at[peers], LAG_STEP)
-    sent(grad_key_ext.at[pl.ds(tokens, 8)], GRAD_EDGE)
+
+    @pl.when(me > 0)
+    def _():
+        sent(grad_key_ext.at[pl.ds(tokens, 8)], GRAD_EDGE)
+
 
     @pl.when(owner)
     def _():

time: 49.4 us -> 49.4 us (level)
  no operation moved by 1% of the time
where the time goes in v7:
time: 49.4 us; the launch traced here: 49.2 us
  Pallas kernels  48.6 us (98%)
  between operations  0.64 us (1%)
    pallas_call x1, Pallas kernels, per_device(): pl.pallas_call(functools.partial(kernel, context, replicas, grad_scale),...  46.4 us
    pallas_call x1, Pallas kernels, per_device(): pl.pallas_call(settle, out_shape=outputs, in_specs=[pl.BlockSpec(memory_s...  2.18 us

profile of v7, /device:TPU:1, one launch (start us, length us, event | category | flops | bytes accessed | tf_op | source)
XLA Modules:
  0.0 49.2 jit_solution(10178289990562134508)
XLA Ops:
  0.6 46.4 %long_convolution_backward.1 = (bf16[1,128,1024]{2,1,0:T(8,128)(2,1)}, bf16[1,128,1024]{2,1,0:T(8,128)(2,1)}, bf16[1,128,1024]{2,1,0:T(8,128)(2,1)}, f32[128,102...) custom-call(bf16[1,128,1024]{2,1,0:T(8,128)(2,1)} %refs_0_.1, bf16[1,128,1024]{2,1,0:T(8,128)(2,1)} %refs_1_.1, ...), custom_call_target="tpu_custom_call" | custom-call | tf_op jit(solution)/shard_map/long_convolution_backward/pallas_call | solution.py:702
  47.0 2.2 %settle.1 = (bf16[1,128,1024]{2,1,0:T(8,128)(2,1)}, bf16[1,128,1024]{2,1,0:T(8,128)(2,1)}, bf16[1,128,1024]{2,1,0:T(8,128)(2,1)}, f32[128,1024]{1,0:T(8,128)}, f32[3,1024]{1,0:T(4,128)}, /*index=5*/f32[1,1024]{1,0:T(1,128)}) custom-call(bf16[1,128,1024]{2,1,0:T(8,128)(2,1)} %get-tuple-element.18.refs_0_, bf16[1,128,1024]{2,1,0:T(8,128)(2,1)} %get-tuple-element.19.refs_1_, ...), custom_call_target="tpu_custom_call" | custom-call | tf_op jit(solution)/shard_map/settle/pallas_call | solution.py:747
